TPU v7x, 256 devices: a whole 4x4x8 slice. The times are simulated.
256 devices in a mesh: slab: 64 (over y_lo, z, x), group: 4 (over y_hi, core).
Axes of the slice: x: 4, y: 4 (y_hi: 2, y_lo: 2; y = y_hi * 2 + y_lo), z: 8, core: 2. Of those that a mesh axis runs over, the one named last changes fastest.
Arguments:
- field_in: bfloat16 [4, 128, 16, 256, 256], P('group', 'slab'), may hold values from -6 to 6
- cotangent: bfloat16 [4, 128, 16, 256, 256], P('group', 'slab'), may hold values from -16 to 16
- weights: bfloat16 [2, 1024, 17, 256], P(None, 'slab'), may hold values from -1.5 to 1.5
Outputs:
- field_grad: bfloat16 [4, 128, 16, 256, 256], P('group', 'slab')
- weight_grad: float32 [2, 1024, 17, 256], P(None, ('slab', 'group'))
All inputs are finite; a program needn't handle non-finite values.
Results may differ from a plain program's by a relative error of at most 0.0042.
Values sent between devices are 32-bit elements; how exact they have to be, the bound alone decides.
No kernel may reach another device: no remote copies, remote signals or barrier semaphores. Data moves between devices by JAX's collectives and lax.ppermute only.
A program may use at most 128 MiB of HBM per device.

v0:
```python
import math

import jax
import jax.numpy as jnp
import ml_dtypes
import numpy as np
from jax import lax
from jax.experimental import pallas as pl
from jax.experimental.pallas import tpu as pltpu
from jax.sharding import PartitionSpec as P

C = 16
KX = 32
KY = 32
KZ = 17
KP = 24
NX = 256
NY = 256
NZ = 128
SLABS = 64
HALF = KY // 2
SCALE = 1.0 / math.sqrt(NX * NY * NZ)
VMEM_LIMIT = 48 * 1024 * 1024

f32 = jnp.float32
bf16 = jnp.bfloat16


def kept_freqs(keep, length):
    index = np.arange(keep)
    return np.where(index < keep // 2, index, length - keep + index)


def phases(positions, freqs, length):
    turns = positions[:, None] * freqs[None, :] % length
    angle = turns.astype(np.float32) * np.float32(2.0 * math.pi / length)
    return angle.astype(np.float64)


def split_np(table):
    table = np.asarray(table, np.float32)
    high = table.astype(ml_dtypes.bfloat16)
    low = (table - high.astype(np.float32)).astype(ml_dtypes.bfloat16)
    return high, low


def x_forward_table():
    angle = phases(np.arange(NX), kept_freqs(KX, NX), NX)
    high, low = split_np(np.concatenate([np.cos(angle), np.sin(angle)], 1).T)
    return np.concatenate([high, low], 0)


def y_forward_table():
    angle = phases(np.arange(NY), kept_freqs(KY, NY), NY)
    real = np.cos(angle).astype(np.float32).astype(ml_dtypes.bfloat16)
    imag = (-np.sin(angle)).astype(np.float32).astype(ml_dtypes.bfloat16)
    parts = []
    for first, second in ((real, imag), (imag, -real)):
        lanes = []
        for half in range(2):
            for part in (first, second):
                cut = part[:, half * HALF:(half + 1) * HALF]
                lanes.extend([cut] * 4)
        parts.append(np.concatenate(lanes, 1))
    return np.concatenate(parts, 0)


def depth_positions():
    s = np.arange(SLABS)
    return np.concatenate([2 * s, 2 * s + 1])


def depth_forward_table():
    angle = phases(depth_positions(), np.arange(KZ), NZ)
    table = np.zeros((2 * KP, NZ), np.float32)
    table[:KZ] = np.cos(angle).T
    table[KP:KP + KZ] = np.sin(angle).T
    high, low = split_np(table)
    return np.concatenate([high, high, low], 1)


def depth_back_table():
    angle = phases(depth_positions(), np.arange(KZ), NZ)
    table = np.zeros((NZ, 2 * KP), np.float32)
    table[:, :KZ] = np.cos(angle)
    table[:, KP:KP + KZ] = np.sin(angle)
    high, low = split_np(table)
    return np.concatenate([high, high, low], 1)


def lane_fields():
    lane = np.arange(512)
    return lane // 128, lane // 64 % 2, lane // 16 % 4, lane % 16


def expand_table(which):
    cg, ri, c4, _ = lane_fields()
    col = np.arange(512)
    col_ri, ci, co = col // 256, col // 16 % 16, col % 16
    target = ci if which == 0 else co
    hit = (ri[:, None] == col_ri[None]) & ((cg * 4 + c4)[:, None] == target[None])
    return hit.astype(ml_dtypes.bfloat16)


def collect_table():
    return np.ascontiguousarray(expand_table(0).T)


def y_back_table():
    angle = phases(kept_freqs(KY, NY), np.arange(NY), NY)
    cos, sin = np.cos(angle), np.sin(angle)
    rows = []
    for half in range(2):
        cut = slice(half * HALF, (half + 1) * HALF)
        rows.extend([np.concatenate([cos[cut], sin[cut]], 1)] * 4)
        rows.extend([np.concatenate([-sin[cut], cos[cut]], 1)] * 4)
    high, low = split_np(np.concatenate(rows, 0))
    return np.concatenate([high, high, low], 0)


def x_back_table():
    angle = phases(np.arange(NX), kept_freqs(KX, NX), NX)
    table = np.concatenate([np.cos(angle), -np.sin(angle)], 1) * SCALE
    high, low = split_np(table)
    return np.concatenate([high, high, low], 1)


def dot(left, right):
    return jnp.dot(left, right, preferred_element_type=f32)


def split(value):
    high = value.astype(bf16)
    low = (value - high.astype(f32)).astype(bf16)
    return high, low


def lane_iota(rows, lanes):
    return lax.broadcasted_iota(jnp.int32, (rows, lanes), 1)


def swap_parts(value):
    tiles = [pltpu.roll(value[:, t * 128:(t + 1) * 128], 64, 1) for t in range(value.shape[1] // 128)]
    return jnp.concatenate(tiles, 1)


def forward_kernel(cot_ref, fld_ref, tx_ref, base_ref, out_ref, v_ref, tm_ref):
    step = pl.program_id(0)
    group = step % 8

    @pl.when(step == 0)
    def _():
        slot = lane_iota(256, 256) // 16 % 4
        for part in range(2):
            base = base_ref[part * 256:(part + 1) * 256, :].astype(f32)
            for c4 in range(4):
                row = (c4 * 2 + part) * 256
                tm_ref[row:row + 256, :] = jnp.where(slot == c4, base, 0.0).astype(bf16)

    def block(ref):
        row = pl.multiple_of(group * 32, 32)
        for c4 in range(4):
            mixed = dot(tx_ref[...], ref[0, 0, c4])
            high, low = split(mixed[:64] + mixed[64:])
            for part in range(2):
                lanes = slice((c4 * 2 + part) * 256, (c4 * 2 + part + 1) * 256)
                v_ref[pl.ds(row, 32), lanes] = high[part * 32:(part + 1) * 32]
                v_ref[pl.ds(row + 256, 32), lanes] = low[part * 32:(part + 1) * 32]

    @pl.when(step < 8)
    def _():
        block(cot_ref)

    @pl.when(step >= 8)
    def _():
        block(fld_ref)

    @pl.when(group == 7)
    def _():
        total = dot(v_ref[...], tm_ref[...])
        total = total[:256] + total[256:]
        first = (step // 8) * 8
        for pg in range(8):
            for half in range(2):
                piece = total[pg * 32:(pg + 1) * 32, half * 128:(half + 1) * 128]
                out_ref[pl.ds(first + half * 16 + pg, 32, stride=32), :] = piece


def forward(cotangent, field_in):
    def cot_map(i):
        j = jnp.minimum(i, 7)
        return (0, j // 4, j % 4, 0, 0)

    def fld_map(i):
        j = jnp.maximum(i - 8, 0)
        return (0, j // 4, j % 4, 0, 0)

    block = (1, 1, 4, NX, NY)
    return pl.pallas_call(
        forward_kernel,
        grid=(16,),
        out_shape=jax.ShapeDtypeStruct((SLABS * 16, 128), f32),
        in_specs=[
            pl.BlockSpec(block, cot_map),
            pl.BlockSpec(block, fld_map),
            pl.BlockSpec((128, NX), lambda i: (0, 0)),
            pl.BlockSpec((512, 256), lambda i: (0, 0)),
        ],
        out_specs=pl.BlockSpec((SLABS * 16, 128), lambda i: (0, 0)),
        scratch_shapes=[pltpu.VMEM((512, 2048), bf16), pltpu.VMEM((2048, 256), bf16)],
        compiler_params=pltpu.CompilerParams(vmem_limit_bytes=VMEM_LIMIT),
        cost_estimate=pl.CostEstimate(flops=4 * 10**9, bytes_accessed=9 * 10**6, transcendentals=0),
        name="forward_planes",
    )(cotangent, field_in, jnp.asarray(x_forward_table()), jnp.asarray(y_forward_table()))


def depth_modes(r_ref, first, tz_ref):
    tiles = []
    for cg in range(4):
        rows = [r_ref[pl.ds(first + p * 4 + cg, SLABS, stride=16), :] for p in range(2)]
        tiles.append(jnp.concatenate(rows, 0))
    high, low = split(jnp.concatenate(tiles, 1))
    both = dot(tz_ref[...], jnp.concatenate([high, low, high], 0))
    cos_part, sin_part = both[:KP], both[KP:]
    sign = jnp.where(lane_iota(KP, 512) % 128 < 64, SCALE, -SCALE)
    return cos_part * SCALE + sign * swap_parts(sin_part)


def spread(values, masks, table):
    rows = jnp.concatenate([jnp.where(mask, value, 0.0) for value, mask in zip(values, masks)], 0)
    high, low = split(rows)
    return dot(high, table) + dot(low, table)


def middle_kernel(r_ref, w_ref, tz_ref, e_ref, c_ref, tb_ref, p_ref, g_ref, prod_ref):
    modes = depth_modes(r_ref, 0, tz_ref)
    g_ref[...] = modes
    ky = lane_iota(KP, 512) % 16
    masks = [ky == m for m in range(HALF)]
    wide = spread([modes] * HALF, masks, e_ref[...])
    prod_ref[...] = jnp.zeros_like(prod_ref)
    for m in range(HALF):
        row = m * KP
        g_real, g_imag = wide[row:row + KZ, :256], wide[row:row + KZ, 256:]
        w_real, w_imag = w_ref[0, m].astype(f32), w_ref[1, m].astype(f32)
        prod_ref[row:row + KZ, :256] = g_real * w_real + g_imag * w_imag
        prod_ref[row:row + KZ, 256:] = g_imag * w_real - g_real * w_imag
    high, low = split(prod_ref[...])
    sums = dot(high, c_ref[...]) + dot(low, c_ref[...])
    direct = jnp.where(masks[0], sums[:KP], 0.0)
    for m in range(1, HALF):
        direct = direct + jnp.where(masks[m], sums[m * KP:(m + 1) * KP], 0.0)
    sign = jnp.where(lane_iota(KP, 512) % 128 < 64, -1.0, 1.0)
    turned = sign * swap_parts(direct)
    high, low = split(jnp.concatenate([direct, turned], 0))
    planes = dot(tb_ref[...], jnp.concatenate([high, low, high], 0))
    for p in range(2):
        for cg in range(4):
            piece = planes[p * SLABS:(p + 1) * SLABS, cg * 128:(cg + 1) * 128]
            p_ref[pl.ds(p * 4 + cg, SLABS, stride=8), :] = piece


def middle(received, weights):
    return pl.pallas_call(
        middle_kernel,
        out_shape=(
            jax.ShapeDtypeStruct((SLABS * 8, 128), f32),
            jax.ShapeDtypeStruct((KP, 512), f32),
        ),
        scratch_shapes=[pltpu.VMEM((HALF * KP, 512), f32)],
        compiler_params=pltpu.CompilerParams(vmem_limit_bytes=VMEM_LIMIT),
        cost_estimate=pl.CostEstimate(flops=2 * 10**9, bytes_accessed=3 * 10**6, transcendentals=0),
        name="middle_modes",
    )(
        received,
        weights,
        jnp.asarray(depth_forward_table()),
        jnp.asarray(expand_table(1)),
        jnp.asarray(collect_table()),
        jnp.asarray(depth_back_table()),
    )


def input_kernel(r_ref, tz_ref, g_ref, out_ref):
    out_ref[:, :512] = depth_modes(r_ref, 8, tz_ref)
    out_ref[:, 512:] = g_ref[...]


def input_modes(received, grad):
    return pl.pallas_call(
        input_kernel,
        out_shape=jax.ShapeDtypeStruct((KP, 1024), f32),
        compiler_params=pltpu.CompilerParams(vmem_limit_bytes=VMEM_LIMIT),
        cost_estimate=pl.CostEstimate(flops=10**8, bytes_accessed=10**6, transcendentals=0),
        name="input_modes",
    )(received, jnp.asarray(depth_forward_table()), grad)


def weight_kernel(own_ref, a_ref, b_ref, c_ref, d_ref, eu_ref, eg_ref, out_ref):
    ky = lane_iota(KP, 512) % 16 - 4 * own_ref[0]
    masks = [ky == m for m in range(4)]
    refs = (a_ref, b_ref, c_ref, d_ref)
    u_all = spread([r[:, :512] for r in refs for _ in range(4)], masks * 4, eu_ref[...])
    g_all = spread([r[:, 512:] for r in refs for _ in range(4)], masks * 4, eg_ref[...])
    for m in range(4):
        real = jnp.zeros((KP, 256), f32)
        imag = jnp.zeros((KP, 256), f32)
        for k in range(4):
            row = (k * 4 + m) * KP
            u_real, u_imag = u_all[row:row + KP, :256], u_all[row:row + KP, 256:]
            g_real, g_imag = g_all[row:row + KP, :256], g_all[row:row + KP, 256:]
            real = real + (u_real * g_real + u_imag * g_imag)
            imag = imag + (u_real * g_imag - u_imag * g_real)
        out_ref[0, m] = real[:KZ]
        out_ref[1, m] = imag[:KZ]


def weight_terms(own, pieces):
    vmem = pl.BlockSpec(memory_space=pltpu.VMEM)
    return pl.pallas_call(
        weight_kernel,
        out_shape=jax.ShapeDtypeStruct((2, 4, KZ, C * C), f32),
        in_specs=[pl.BlockSpec(memory_space=pltpu.SMEM)] + [vmem] * 6,
        out_specs=vmem,
        compiler_params=pltpu.CompilerParams(vmem_limit_bytes=VMEM_LIMIT),
        cost_estimate=pl.CostEstimate(flops=2 * 10**9, bytes_accessed=2 * 10**6, transcendentals=0),
        name="weight_terms",
    )(own, *pieces, jnp.asarray(expand_table(0)), jnp.asarray(expand_table(1)))


def back_kernel(r_ref, ty_ref, tx_ref, out_ref, q_ref):
    step = pl.program_id(0)

    @pl.when(step == 0)
    def _():
        rows = []
        for pg in range(8):
            halves = [r_ref[pl.ds(half * 8 + pg, KX, stride=16), :] for half in range(2)]
            rows.append(jnp.concatenate(halves, 1))
        grid = jnp.concatenate(rows, 0)
        slot = lane_iota(256, 256) // 16 % 4
        for c4 in range(4):
            high, low = split(jnp.where(slot == c4, grid, 0.0))
            mixed = dot(jnp.concatenate([high, low, high], 1), ty_ref[...])
            high, low = split(mixed)
            for pg in range(8):
                for part in range(2):
                    cut = (slice(pg * 32, (pg + 1) * 32), slice(part * 256, (part + 1) * 256))
                    q_ref[pg * 4 + c4, part * 32:(part + 1) * 32, :] = high[cut]
                    q_ref[pg * 4 + c4, 64 + part * 32:64 + (part + 1) * 32, :] = low[cut]

    for c4 in range(4):
        q = q_ref[step * 4 + c4]
        field = dot(tx_ref[...], jnp.concatenate([q, q[:64]], 0))
        out_ref[0, 0, c4] = field.astype(bf16)


def back(received):
    return pl.pallas_call(
        back_kernel,
        grid=(8,),
        out_shape=jax.ShapeDtypeStruct((1, 2, C, NX, NY), bf16),
        in_specs=[
            pl.BlockSpec((SLABS * 8, 128), lambda i: (0, 0)),
            pl.BlockSpec((768, 512), lambda i: (0, 0)),
            pl.BlockSpec((NX, 192), lambda i: (0, 0)),
        ],
        out_specs=pl.BlockSpec((1, 1, 4, NX, NY), lambda i: (0, i // 4, i % 4, 0, 0)),
        scratch_shapes=[pltpu.VMEM((32, 128, 256), bf16)],
        compiler_params=pltpu.CompilerParams(vmem_limit_bytes=VMEM_LIMIT),
        cost_estimate=pl.CostEstimate(flops=4 * 10**9, bytes_accessed=6 * 10**6, transcendentals=0),
        name="back_planes",
    )(received, jnp.asarray(y_back_table()), jnp.asarray(x_back_table()))


def exchange(chunks, rows):
    moved = lax.all_to_all(chunks.reshape(SLABS, rows, 128), "slab", 0, 0, tiled=True)
    return moved.reshape(SLABS * rows, 128)


def body(field_in, cotangent, weights):
    received = exchange(forward(cotangent, field_in), 16)
    planes, grad = middle(received, weights)
    returned = exchange(planes, 8)
    own = input_modes(received, grad)
    pieces = [own]
    for k in range(1, 4):
        pieces.append(lax.ppermute(own, "group", [(i, i ^ k) for i in range(4)]))
    index = lax.axis_index("group").astype(jnp.int32).reshape(1)
    weight_grad = weight_terms(index, pieces)
    return (back(returned), weight_grad)


def solution(mesh):
    in_specs = (
        P("group", "slab", None, None, None),
        P("group", "slab", None, None, None),
        P(None, "slab", None, None),
    )
    out_specs = (P("group", "slab", None, None, None), P(None, ("slab", "group"), None, None))
    return jax.shard_map(body, mesh=mesh, in_specs=in_specs, out_specs=out_specs, check_vma=False)
```

profile of v0, /device:TPU:1, one launch (start us, length us, event | category | flops | bytes accessed | tf_op | source)
XLA Modules:
  0.0 74.8 jit_solution(14577153974986747013)
XLA Ops:
  0.6 0.0 copy-start
  0.6 0.0 copy-start.1
  0.7 2.2 %copy-done.1 = bf16[1,2,16,256,256]{4,3,2,1,0:T(8,128)(2,1)S(1)} copy-done((bf16[1,2,16,256,256]{4,3,2,1,0:T(8,128)(2,1)S(1)}, bf16[1,2,16,256,256]{4,3,2,1,0:T(8,128)(2,1)}, u32[]{:S(2)}) %copy-start.1) | copy-done | bytes 4194328
  2.8 0.0 copy-start.6
  2.8 0.9 %copy-done.6 = bf16[512,256]{1,0:T(8,128)(2,1)S(1)} copy-done((bf16[512,256]{1,0:T(8,128)(2,1)S(1)}, bf16[512,256]{1,0:T(8,128)(2,1)}, u32[]{:S(2)}) %copy-start.6) | copy-done | bytes 262168
  3.8 0.0 copy-start.9
  3.8 0.8 %copy-done.9 = bf16[128,256]{1,0:T(8,128)(2,1)S(1)} copy-done((bf16[128,256]{1,0:T(8,128)(2,1)S(1)}, bf16[128,256]{1,0:T(8,128)(2,1)}, u32[]{:S(2)}) %copy-start.9) | copy-done | bytes 65560
  4.6 0.0 copy-start.10
  4.6 0.0 copy-start.3
  4.6 0.0 copy-start.5
  4.6 0.0 copy-start.8
  4.6 11.3 %forward_planes.1 = f32[1024,128]{1,0:T(8,128)} custom-call(bf16[1,2,16,256,256]{4,3,2,1,0:T(8,128)(2,1)S(1)} %copy-done.1, bf16[1,2,16,256,256]{4,3,2,1,0:T(8,128)(2,1)} %fld_ref.1, bf16[128,256]{1,0:T(8,128)(2,1)S(1)} %copy-done.9, bf16[512,256]{1,0:T(8,128)(2,1)S(1)} %copy-done.6), custom_call_target="tpu_custom_call" | custom-call | flops 4000000000 | bytes 9000000 | tf_op jit(solution)/shard_map/forward_planes/pallas_call | solution.py:199
  16.0 13.5 %all-to-all-start = ((f32[64,16,128]{2,1,0:T(8,128)}), f32[64,16,128]{2,1,0:T(8,128)S(1)}, u32[]{:S(2)}, u32[]{:S(2)}) async-start(f32[64,16,128]{2,1,0:T(8,128)} %bitcast), calls=%async_computation | async-start | bytes 1048576 | tf_op jit(solution)/shard_map/all_to_all | solution.py:377
  29.5 0.0 copy-done.10
  29.5 0.1 copy.16.w_ref
  29.6 15.8 %all-to-all-done = f32[64,16,128]{2,1,0:T(8,128)S(1)} async-done(((f32[64,16,128]{2,1,0:T(8,128)}), f32[64,16,128]{2,1,0:T(8,128)S(1)}, u32[]{:S(2)}, u32[]{:S(2)}) %all-to-all-start) | async-done | bytes 524320 | tf_op jit(solution)/shard_map/all_to_all | solution.py:377
  45.4 0.0 copy-done
  45.4 0.0 copy-done.3
  45.4 0.0 copy-done.5
  45.4 0.0 copy-done.8
  45.4 0.0 copy-start.4
  45.4 2.4 %middle_modes.1 = (f32[512,128]{1,0:T(8,128)}, f32[24,512]{1,0:T(8,128)S(1)}) custom-call(f32[1024,128]{1,0:T(8,128)S(1)} %bitcast.5, bf16[2,16,17,256]{3,2,1,0:T(8,128)(2,1)S(1)} %copy.16.w_ref, bf16[48,384]{1,0:T(8,128)(2,1)S(1)} %copy-done, bf16[512,512]{1,0:T(8,128)(2,1)S(1)} %copy-done.3, bf16[512,512]{1,0:T(8,128)(2,1)S(1)} %copy-done.5, ...), custom_call_target="tpu_custom_call" | custom-call | flops 2000000000 | bytes 3000000 | tf_op jit(solution)/shard_map/middle_modes/pallas_call | solution.py:264
  47.8 6.9 %all-to-all-start.1 = ((f32[64,8,128]{2,1,0:T(8,128)}), f32[64,8,128]{2,1,0:T(8,128)S(1)}, u32[]{:S(2)}, u32[]{:S(2)}) async-start(f32[64,8,128]{2,1,0:T(8,128)} %bitcast.2), calls=%async_computation.1 | async-start | bytes 524288 | tf_op jit(solution)/shard_map/all_to_all | solution.py:377
  54.7 0.0 copy-start.2
  54.7 0.0 copy-start.7
  54.7 0.3 input_modes.1.a_ref
  55.1 4.3 %collective-permute-start.2 = (f32[24,1024]{1,0:T(8,128)S(1)}, f32[24,1024]{1,0:T(8,128)S(1)}, u32[]{:S(2)}, u32[]{:S(2)}) collective-permute-start(f32[24,1024]{1,0:T(8,128)S(1)} %input_modes.1.a_ref), channel_id=1, source_target_pairs={{0,3},{1,2},{2,1},{3,0},{4,7},{5,6},{6,5},{7,4},{8,11},{9,10},{10,... | collective-permute-start | bytes 294920 | tf_op jit(solution)/shard_map/ppermute | solution.py:388
  59.4 0.3 collective-permute-start.1
  59.7 0.1 collective-permute-start
  59.9 4.2 %collective-permute-done.2.d_ref = f32[24,1024]{1,0:T(8,128)S(1)} collective-permute-done((f32[24,1024]{1,0:T(8,128)S(1)}, f32[24,1024]{1,0:T(8,128)S(1)}, u32[]{:S(2)}, u32[]{:S(2)}) %collective-permute-start.2) | collective-permute-done | bytes 98336 | tf_op jit(solution)/shard_map/ppermute | solution.py:388
  64.0 3.2 %collective-permute-done.1.c_ref = f32[24,1024]{1,0:T(8,128)S(1)} collective-permute-done((f32[24,1024]{1,0:T(8,128)S(1)}, f32[24,1024]{1,0:T(8,128)S(1)}, u32[]{:S(2)}, u32[]{:S(2)}) %collective-permute-start.1) | collective-permute-done | bytes 98336 | tf_op jit(solution)/shard_map/ppermute | solution.py:388
  67.2 0.0 collective-permute-done.b_ref
  67.2 0.0 copy-done.4
  67.2 1.0 %weight_terms.1 = f32[2,4,17,256]{3,2,1,0:T(8,128)S(1)} custom-call(s32[1]{0:T(128)} %bitcast.4.own_ref, f32[24,1024]{1,0:T(8,128)S(1)} %input_modes.1.a_ref, f32[24,1024]{1,0:T(8,128)S(1)} %collective-permute-done.b_ref, f32[24,1024]{1,0:T(8,128)S(1)} %collective-permute-done.1.c_ref, f32[24,1024]{1,0:T(8,128)S(1)} %collective-permute-done.2.d_ref, ...), custom_call_target="tpu_custom_call" | custom-call | flops 2000000000 | bytes 2000000 | tf_op jit(solution)/shard_map/weight_terms/pallas_call | solution.py:320
  68.2 0.7 copy.17
  69.0 0.0 all-to-all-done.1
  69.0 0.0 copy-done.2
  69.0 0.0 copy-done.7
  69.0 5.8 %back_planes.1 = bf16[1,2,16,256,256]{4,3,2,1,0:T(8,128)(2,1)} custom-call(f32[512,128]{1,0:T(8,128)S(1)} %bitcast.7, bf16[768,512]{1,0:T(8,128)(2,1)S(1)} %copy-done.2, bf16[256,192]{1,0:T(8,128)(2,1)S(1)} %copy-done.7), custom_call_target="tpu_custom_call" | custom-call | flops 4000000000 | bytes 6000000 | tf_op jit(solution)/shard_map/back_planes/pallas_call | solution.py:359
Async XLA Ops:
  0.6 44.8 %copy-start = (bf16[48,384]{1,0:T(8,128)(2,1)S(1)}, bf16[48,384]{1,0:T(8,128)(2,1)}, u32[]{:S(2)}) copy-start(bf16[48,384]{1,0:T(8,128)(2,1)} %constant.24.clone.tz_ref) | copy-start | bytes 110596
  0.6 2.2 %copy-start.1 = (bf16[1,2,16,256,256]{4,3,2,1,0:T(8,128)(2,1)S(1)}, bf16[1,2,16,256,256]{4,3,2,1,0:T(8,128)(2,1)}, u32[]{:S(2)}) copy-start(bf16[1,2,16,256,256]{4,3,2,1,0:T(8,128)(2,1)} %cot_ref.1) | copy-start | bytes 12582916
  2.8 0.9 %copy-start.6 = (bf16[512,256]{1,0:T(8,128)(2,1)S(1)}, bf16[512,256]{1,0:T(8,128)(2,1)}, u32[]{:S(2)}) copy-start(bf16[512,256]{1,0:T(8,128)(2,1)} %constant.23.clone.base_ref) | copy-start | bytes 786436
  3.8 0.8 %copy-start.9 = (bf16[128,256]{1,0:T(8,128)(2,1)S(1)}, bf16[128,256]{1,0:T(8,128)(2,1)}, u32[]{:S(2)}) copy-start(bf16[128,256]{1,0:T(8,128)(2,1)} %constant.22.clone.tx_ref) | copy-start | bytes 196612
  4.6 24.8 %copy-start.10 = (bf16[2,16,17,256]{3,1,2,0:T(8,128)(2,1)S(1)}, bf16[2,16,17,256]{3,1,2,0:T(8,128)(2,1)}, u32[]{:S(2)}) copy-start(bf16[2,16,17,256]{3,1,2,0:T(8,128)(2,1)} %param.16) | copy-start | bytes 835588
  4.6 40.8 %copy-start.3 = (bf16[512,512]{1,0:T(8,128)(2,1)S(1)}, bf16[512,512]{1,0:T(8,128)(2,1)}, u32[]{:S(2)}) copy-start(bf16[512,512]{1,0:T(8,128)(2,1)} %constant.25.clone.e_ref.eg_ref) | copy-start | bytes 1572868
  4.6 40.8 %copy-start.5 = (bf16[512,512]{1,0:T(8,128)(2,1)S(1)}, bf16[512,512]{1,0:T(8,128)(2,1)}, u32[]{:S(2)}) copy-start(bf16[512,512]{1,0:T(8,128)(2,1)} %constant.26.clone.c_ref) | copy-start | bytes 1572868
  4.6 40.8 %copy-start.8 = (bf16[128,144]{1,0:T(8,128)(2,1)S(1)}, bf16[128,144]{1,0:T(8,128)(2,1)}, u32[]{:S(2)}) copy-start(bf16[128,144]{1,0:T(8,128)(2,1)} %constant.27.clone.tb_ref) | copy-start | bytes 110596
  16.0 29.4 %all-to-all-start = ((f32[64,16,128]{2,1,0:T(8,128)}), f32[64,16,128]{2,1,0:T(8,128)S(1)}, u32[]{:S(2)}, u32[]{:S(2)}) async-start(f32[64,16,128]{2,1,0:T(8,128)} %bitcast), calls=%async_computation | async-start | bytes 1048576 | tf_op jit(solution)/shard_map/all_to_all | solution.py:377
  45.4 21.8 %copy-start.4 = (bf16[512,512]{1,0:T(8,128)(2,1)S(1)}, bf16[512,512]{1,0:T(8,128)(2,1)}, u32[]{:S(2)}) copy-start(bf16[512,512]{1,0:T(8,128)(2,1)} %constant.28.clone.eu_ref) | copy-start | bytes 1572868
  47.8 21.2 %all-to-all-start.1 = ((f32[64,8,128]{2,1,0:T(8,128)}), f32[64,8,128]{2,1,0:T(8,128)S(1)}, u32[]{:S(2)}, u32[]{:S(2)}) async-start(f32[64,8,128]{2,1,0:T(8,128)} %bitcast.2), calls=%async_computation.1 | async-start | bytes 524288 | tf_op jit(solution)/shard_map/all_to_all | solution.py:377
  54.7 14.2 %copy-start.2 = (bf16[768,512]{1,0:T(8,128)(2,1)S(1)}, bf16[768,512]{1,0:T(8,128)(2,1)}, u32[]{:S(2)}) copy-start(bf16[768,512]{1,0:T(8,128)(2,1)} %constant.29.clone.ty_ref) | copy-start | bytes 2359300
  54.7 14.2 %copy-start.7 = (bf16[256,192]{1,0:T(8,128)(2,1)S(1)}, bf16[256,192]{1,0:T(8,128)(2,1)}, u32[]{:S(2)}) copy-start(bf16[256,192]{1,0:T(8,128)(2,1)} %constant.30.clone.tx_ref) | copy-start | bytes 294916
  55.1 8.9 %collective-permute-start.2 = (f32[24,1024]{1,0:T(8,128)S(1)}, f32[24,1024]{1,0:T(8,128)S(1)}, u32[]{:S(2)}, u32[]{:S(2)}) collective-permute-start(f32[24,1024]{1,0:T(8,128)S(1)} %input_modes.1.a_ref), channel_id=1, source_target_pairs={{0,3},{1,2},{2,1},{3,0},{4,7},{5,6},{6,5},{7,4},{8,11},{9,10},{10,... | collective-permute-start | bytes 294920 | tf_op jit(solution)/shard_map/ppermute | solution.py:388
  59.4 7.9 %collective-permute-start.1 = (f32[24,1024]{1,0:T(8,128)S(1)}, f32[24,1024]{1,0:T(8,128)S(1)}, u32[]{:S(2)}, u32[]{:S(2)}) collective-permute-start(f32[24,1024]{1,0:T(8,128)S(1)} %input_modes.1.a_ref), channel_id=1, source_target_pairs={{0,2},{1,3},{2,0},{3,1},{4,6},{5,7},{6,4},{7,5},{8,10},{9,11},{10,... | collective-permute-start | bytes 294920 | tf_op jit(solution)/shard_map/ppermute | solution.py:388
  59.7 7.5 %collective-permute-start = (f32[24,1024]{1,0:T(8,128)S(1)}, f32[24,1024]{1,0:T(8,128)S(1)}, u32[]{:S(2)}, u32[]{:S(2)}) collective-permute-start(f32[24,1024]{1,0:T(8,128)S(1)} %input_modes.1.a_ref), channel_id=1, source_target_pairs={{0,1},{1,0},{2,3},{3,2},{4,5},{5,4},{6,7},{7,6},{8,9},{9,8},{10,11... | collective-permute-start | bytes 294920 | tf_op jit(solution)/shard_map/ppermute | solution.py:388
where the time goes:
time: 75.2 us; the launch traced here: 74.8 us
  starting transfers between devices  25.2 us (34%)
  waiting for transfers between devices  23.2 us (31%)
  Pallas kernels  20.8 us (28%)
  local copies, waits for them, and re-layouts  4.83 us (6%)
    all_to_all x2, starting transfers between devices, exchange(): lax.all_to_all(chunks.reshape(SLABS, rows, 128), 'slab', 0, 0, tiled=True)  20.4 us
    all_to_all x2, waiting for transfers between devices, exchange(): lax.all_to_all(chunks.reshape(SLABS, rows, 128), 'slab', 0, 0, tiled=True)  15.8 us
    pallas_call x1, Pallas kernels, forward(): pl.pallas_call(forward_kernel, grid=(16,), out_shape=jax.ShapeDtypeStruct...  11.3 us
    ppermute x3, waiting for transfers between devices, body(): pieces.append(lax.ppermute(own, 'group', [(i, i ^ k) for i in range(4)]))  7.37 us
    pallas_call x1, Pallas kernels, back(): pl.pallas_call(back_kernel, grid=(8,), out_shape=jax.ShapeDtypeStruct((1,...  5.78 us
    unnamed x24, local copies, waits for them, and re-layouts  4.83 us
    ppermute x3, starting transfers between devices, body(): pieces.append(lax.ppermute(own, 'group', [(i, i ^ k) for i in range(4)]))  4.78 us
    pallas_call x1, Pallas kernels, middle(): pl.pallas_call(middle_kernel, out_shape=(jax.ShapeDtypeStruct((SLABS * 8,...  2.35 us
  transfers between devices with their start and end apart: 5, of which 3 were waited for; matrix products, arithmetic and copies ran while one was open for 1% of the time, Pallas kernels for 2%

commit v1 on v0

--- a/solution.py
+++ b/solution.py
@@ -54,15 +54,11 @@
     angle = phases(np.arange(NY), kept_freqs(KY, NY), NY)
     real = np.cos(angle).astype(np.float32).astype(ml_dtypes.bfloat16)
     imag = (-np.sin(angle)).astype(np.float32).astype(ml_dtypes.bfloat16)
-    parts = []
-    for first, second in ((real, imag), (imag, -real)):
-        lanes = []
-        for half in range(2):
-            for part in (first, second):
-                cut = part[:, half * HALF:(half + 1) * HALF]
-                lanes.extend([cut] * 4)
-        parts.append(np.concatenate(lanes, 1))
-    return np.concatenate(parts, 0)
+    lanes = []
+    for half in range(2):
+        for part in (real, imag):
+            lanes.extend([part[:, half * HALF:(half + 1) * HALF]] * 4)
+    return np.concatenate(lanes, 1)
 
 
 def depth_positions():
@@ -115,7 +111,7 @@
         rows.extend([np.concatenate([cos[cut], sin[cut]], 1)] * 4)
         rows.extend([np.concatenate([-sin[cut], cos[cut]], 1)] * 4)
     high, low = split_np(np.concatenate(rows, 0))
-    return np.concatenate([high, high, low], 0)
+    return np.concatenate([high, low], 0)
 
 
 def x_back_table():
@@ -144,74 +140,74 @@
     return jnp.concatenate(tiles, 1)
 
 
-def forward_kernel(cot_ref, fld_ref, tx_ref, base_ref, out_ref, v_ref, tm_ref):
-    step = pl.program_id(0)
-    group = step % 8
-
-    @pl.when(step == 0)
-    def _():
-        slot = lane_iota(256, 256) // 16 % 4
-        for part in range(2):
-            base = base_ref[part * 256:(part + 1) * 256, :].astype(f32)
-            for c4 in range(4):
-                row = (c4 * 2 + part) * 256
-                tm_ref[row:row + 256, :] = jnp.where(slot == c4, base, 0.0).astype(bf16)
-
-    def block(ref):
-        row = pl.multiple_of(group * 32, 32)
-        for c4 in range(4):
-            mixed = dot(tx_ref[...], ref[0, 0, c4])
-            high, low = split(mixed[:64] + mixed[64:])
-            for part in range(2):
-                lanes = slice((c4 * 2 + part) * 256, (c4 * 2 + part + 1) * 256)
-                v_ref[pl.ds(row, 32), lanes] = high[part * 32:(part + 1) * 32]
-                v_ref[pl.ds(row + 256, 32), lanes] = low[part * 32:(part + 1) * 32]
-
-    @pl.when(step < 8)
-    def _():
-        block(cot_ref)
-
-    @pl.when(step >= 8)
-    def _():
-        block(fld_ref)
-
-    @pl.when(group == 7)
-    def _():
-        total = dot(v_ref[...], tm_ref[...])
-        total = total[:256] + total[256:]
-        first = (step // 8) * 8
-        for pg in range(8):
-            for half in range(2):
-                piece = total[pg * 32:(pg + 1) * 32, half * 128:(half + 1) * 128]
-                out_ref[pl.ds(first + half * 16 + pg, 32, stride=32), :] = piece
+STEPS = 16
+WAITS = (1, 1, 2, 4, 8)
+
+
+def forward_kernel(cot_hbm, fld_hbm, tx_hbm, ty_hbm, out_ref, field_ref, tx_ref, ty_ref, rows_ref, sems):
+    tables = [
+        pltpu.make_async_copy(ty_hbm, ty_ref, sems.at[STEPS]),
+        pltpu.make_async_copy(tx_hbm, tx_ref, sems.at[STEPS + 1]),
+    ]
+    blocks = []
+    for i in range(STEPS):
+        source = cot_hbm if i < 8 else fld_hbm
+        blocks.append(pltpu.make_async_copy(source.at[pl.ds(i % 8 * 4, 4)], field_ref.at[pl.ds(i * 4, 4)], sems.at[i]))
+    for copy in tables + blocks:
+        copy.start()
+    for copy in tables:
+        copy.wait()
+    slot = lane_iota(NX, 256) // 16 % 4
+    sign = jnp.where(lane_iota(KX, 256) % 128 < 64, 1.0, -1.0)
+
+    def rows_y(i):
+        parts = [dot(field_ref[i * 4 + c4], ty_ref[...]) for c4 in range(4)]
+        rows = jnp.where(slot == 0, parts[0], jnp.where(slot == 1, parts[1], jnp.where(slot == 2, parts[2], parts[3])))
+        high, low = split(rows)
+        rows_ref[i % 2, 0] = high
+        rows_ref[i % 2, 1] = low
+
+    def spectrum(i):
+        mixed = dot(tx_ref[...], rows_ref[i % 2, 0])
+        mixed = mixed[:64] + mixed[64:] + dot(tx_ref[:64], rows_ref[i % 2, 1])
+        result = mixed[:KX] + sign * swap_parts(mixed[KX:])
+        for half in range(2):
+            out_ref[pl.ds(half * 16 + i, KX, stride=32), :] = result[:, half * 128:(half + 1) * 128]
+
+    first = 0
+    for count in WAITS:
+        for i in range(first, first + count):
+            blocks[i].wait()
+        for i in range(first, first + count):
+            rows_y(i)
+            if i > 0:
+                spectrum(i - 1)
+        first += count
+    spectrum(STEPS - 1)
 
 
 def forward(cotangent, field_in):
-    def cot_map(i):
-        j = jnp.minimum(i, 7)
-        return (0, j // 4, j % 4, 0, 0)
-
-    def fld_map(i):
-        j = jnp.maximum(i - 8, 0)
-        return (0, j // 4, j % 4, 0, 0)
-
-    block = (1, 1, 4, NX, NY)
+    anywhere = pl.BlockSpec(memory_space=pl.ANY)
     return pl.pallas_call(
         forward_kernel,
-        grid=(16,),
         out_shape=jax.ShapeDtypeStruct((SLABS * 16, 128), f32),
-        in_specs=[
-            pl.BlockSpec(block, cot_map),
-            pl.BlockSpec(block, fld_map),
-            pl.BlockSpec((128, NX), lambda i: (0, 0)),
-            pl.BlockSpec((512, 256), lambda i: (0, 0)),
+        in_specs=[anywhere] * 4,
+        scratch_shapes=[
+            pltpu.VMEM((STEPS * 4, NX, NY), bf16),
+            pltpu.VMEM((128, NX), bf16),
+            pltpu.VMEM((NY, 256), bf16),
+            pltpu.VMEM((2, 2, NX, 256), bf16),
+            pltpu.SemaphoreType.DMA((STEPS + 2,)),
         ],
-        out_specs=pl.BlockSpec((SLABS * 16, 128), lambda i: (0, 0)),
-        scratch_shapes=[pltpu.VMEM((512, 2048), bf16), pltpu.VMEM((2048, 256), bf16)],
-        compiler_params=pltpu.CompilerParams(vmem_limit_bytes=VMEM_LIMIT),
+        compiler_params=pltpu.CompilerParams(vmem_limit_bytes=60 * 1024 * 1024),
         cost_estimate=pl.CostEstimate(flops=4 * 10**9, bytes_accessed=9 * 10**6, transcendentals=0),
         name="forward_planes",
-    )(cotangent, field_in, jnp.asarray(x_forward_table()), jnp.asarray(y_forward_table()))
+    )(
+        cotangent.reshape(2 * C, NX, NY),
+        field_in.reshape(2 * C, NX, NY),
+        jnp.asarray(x_forward_table()),
+        jnp.asarray(y_forward_table()),
+    )
 
 
 def depth_modes(r_ref, first, tz_ref):
@@ -311,66 +307,72 @@
             g_real, g_imag = g_all[row:row + KP, :256], g_all[row:row + KP, 256:]
             real = real + (u_real * g_real + u_imag * g_imag)
             imag = imag + (u_real * g_imag - u_imag * g_real)
-        out_ref[0, m] = real[:KZ]
-        out_ref[1, m] = imag[:KZ]
+        out_ref[0, :, m, :] = real[:KZ]
+        out_ref[1, :, m, :] = imag[:KZ]
 
 
 def weight_terms(own, pieces):
     vmem = pl.BlockSpec(memory_space=pltpu.VMEM)
-    return pl.pallas_call(
+    terms = pl.pallas_call(
         weight_kernel,
-        out_shape=jax.ShapeDtypeStruct((2, 4, KZ, C * C), f32),
+        out_shape=jax.ShapeDtypeStruct((2, KZ, 4, C * C), f32),
         in_specs=[pl.BlockSpec(memory_space=pltpu.SMEM)] + [vmem] * 6,
         out_specs=vmem,
         compiler_params=pltpu.CompilerParams(vmem_limit_bytes=VMEM_LIMIT),
         cost_estimate=pl.CostEstimate(flops=2 * 10**9, bytes_accessed=2 * 10**6, transcendentals=0),
         name="weight_terms",
     )(own, *pieces, jnp.asarray(expand_table(0)), jnp.asarray(expand_table(1)))
-
-
-def back_kernel(r_ref, ty_ref, tx_ref, out_ref, q_ref):
-    step = pl.program_id(0)
-
-    @pl.when(step == 0)
-    def _():
-        rows = []
+    return terms.transpose(0, 2, 1, 3)
+
+
+def back_kernel(r_ref, ty_ref, tx_ref, out_hbm, field_ref, q_ref, sems):
+    rows = []
+    for pg in range(8):
+        halves = [r_ref[pl.ds(half * 8 + pg, KX, stride=16), :] for half in range(2)]
+        rows.append(jnp.concatenate(halves, 1))
+    grid = jnp.concatenate(rows, 0)
+    slot = lane_iota(256, 256) // 16 % 4
+
+    def rows_x(c4):
+        high, low = split(jnp.where(slot == c4, grid, 0.0))
+        mixed = dot(jnp.concatenate([high, low], 0), ty_ref[:256])
+        mixed = mixed[:256] + mixed[256:] + dot(high, ty_ref[256:])
+        high, low = split(mixed)
         for pg in range(8):
-            halves = [r_ref[pl.ds(half * 8 + pg, KX, stride=16), :] for half in range(2)]
-            rows.append(jnp.concatenate(halves, 1))
-        grid = jnp.concatenate(rows, 0)
-        slot = lane_iota(256, 256) // 16 % 4
-        for c4 in range(4):
-            high, low = split(jnp.where(slot == c4, grid, 0.0))
-            mixed = dot(jnp.concatenate([high, low, high], 1), ty_ref[...])
-            high, low = split(mixed)
-            for pg in range(8):
-                for part in range(2):
-                    cut = (slice(pg * 32, (pg + 1) * 32), slice(part * 256, (part + 1) * 256))
-                    q_ref[pg * 4 + c4, part * 32:(part + 1) * 32, :] = high[cut]
-                    q_ref[pg * 4 + c4, 64 + part * 32:64 + (part + 1) * 32, :] = low[cut]
-
+            for part in range(2):
+                cut = (slice(pg * 32, (pg + 1) * 32), slice(part * 256, (part + 1) * 256))
+                q_ref[c4, pg, part * 32:(part + 1) * 32, :] = high[cut]
+                q_ref[c4, pg, 64 + part * 32:64 + (part + 1) * 32, :] = low[cut]
+
+    copies = []
+    rows_x(0)
     for c4 in range(4):
-        q = q_ref[step * 4 + c4]
-        field = dot(tx_ref[...], jnp.concatenate([q, q[:64]], 0))
-        out_ref[0, 0, c4] = field.astype(bf16)
+        if c4 < 3:
+            rows_x(c4 + 1)
+        for pg in range(8):
+            q = q_ref[c4, pg]
+            field_ref[pg, c4] = dot(tx_ref[...], jnp.concatenate([q, q[:64]], 0)).astype(bf16)
+            copies.append(pltpu.make_async_copy(field_ref.at[pg, c4], out_hbm.at[pg, c4], sems.at[c4 * 8 + pg]))
+            copies[-1].start()
+    for copy in copies:
+        copy.wait()
 
 
 def back(received):
-    return pl.pallas_call(
+    field = pl.pallas_call(
         back_kernel,
-        grid=(8,),
-        out_shape=jax.ShapeDtypeStruct((1, 2, C, NX, NY), bf16),
-        in_specs=[
-            pl.BlockSpec((SLABS * 8, 128), lambda i: (0, 0)),
-            pl.BlockSpec((768, 512), lambda i: (0, 0)),
-            pl.BlockSpec((NX, 192), lambda i: (0, 0)),
+        out_shape=jax.ShapeDtypeStruct((8, 4, NX, NY), bf16),
+        out_specs=pl.BlockSpec(memory_space=pl.ANY),
+        scratch_shapes=[
+            pltpu.VMEM((8, 4, NX, NY), bf16),
+            pltpu.VMEM((4, 8, 128, NY), bf16),
+            pltpu.SemaphoreType.DMA((32,)),
         ],
-        out_specs=pl.BlockSpec((1, 1, 4, NX, NY), lambda i: (0, i // 4, i % 4, 0, 0)),
-        scratch_shapes=[pltpu.VMEM((32, 128, 256), bf16)],
         compiler_params=pltpu.CompilerParams(vmem_limit_bytes=VMEM_LIMIT),
         cost_estimate=pl.CostEstimate(flops=4 * 10**9, bytes_accessed=6 * 10**6, transcendentals=0),
         name="back_planes",
     )(received, jnp.asarray(y_back_table()), jnp.asarray(x_back_table()))
+    return field.reshape(1, 2, C, NX, NY)
 
 
 def exchange(chunks, rows):
@@ -387,8 +389,9 @@
     for k in range(1, 4):
         pieces.append(lax.ppermute(own, "group", [(i, i ^ k) for i in range(4)]))
     index = lax.axis_index("group").astype(jnp.int32).reshape(1)
-    weight_grad = weight_terms(index, pieces)
-    return (back(returned), weight_grad)
+    field_grad = back(returned)
+    pieces, field_grad = lax.optimization_barrier((pieces, field_grad))
+    return (field_grad, weight_terms(index, pieces))
 
 
 def solution(mesh):

time: 75.2 us -> 63.8 us (0.85)
  the two profiles are of different devices: /device:TPU:1 before, /device:TPU:16 now
where the time goes in v1:
time: 63.8 us; the launch traced here: 63.5 us
  waiting for transfers between devices  26.2 us (41%)
  starting transfers between devices  22.2 us (35%)
  Pallas kernels  14.2 us (22%)
  between operations  0.8 us (1%)
    all_to_all x2, waiting for transfers between devices, exchange(): lax.all_to_all(chunks.reshape(SLABS, rows, 128), 'slab', 0, 0, tiled=True)  26.2 us
    all_to_all x2, starting transfers between devices, exchange(): lax.all_to_all(chunks.reshape(SLABS, rows, 128), 'slab', 0, 0, tiled=True)  18.7 us
    pallas_call x1, Pallas kernels, forward(): pl.pallas_call(forward_kernel, out_shape=jax.ShapeDtypeStruct((SLABS * 16...  6.62 us
    ppermute x3, starting transfers between devices, body(): pieces.append(lax.ppermute(own, 'group', [(i, i ^ k) for i in range(4)]))  3.46 us
    pallas_call x1, Pallas kernels, back(): pl.pallas_call(back_kernel, out_shape=jax.ShapeDtypeStruct((8, 4, NX, NY)...  3.22 us
    pallas_call x1, Pallas kernels, middle(): pl.pallas_call(middle_kernel, out_shape=(jax.ShapeDtypeStruct((SLABS * 8,...  2.34 us
    pallas_call x1, Pallas kernels, weight_terms(): pl.pallas_call(weight_kernel, out_shape=jax.ShapeDtypeStruct((2, KZ, 4, C...  1.7 us
  transfers between devices with their start and end apart: 5, of which 2 were waited for; matrix products, arithmetic and copies ran while one was open for 0% of the time, Pallas kernels for 6%

profile of v1, /device:TPU:16, one launch (start us, length us, event | category | flops | bytes accessed | tf_op | source)
XLA Modules:
  0.0 63.5 jit_solution(8034905245350840748)
XLA Ops:
  0.6 0.0 copy-start.7
  0.6 0.0 copy-start
  0.7 0.0 copy-start.1
  0.7 0.0 copy-start.4
  0.7 0.0 copy-start.6
  0.7 6.6 %forward_planes.1 = f32[1024,128]{1,0:T(8,128)} custom-call(bf16[32,256,256]{2,1,0:T(8,128)(2,1)} %bitcast.13, bf16[32,256,256]{2,1,0:T(8,128)(2,1)} %bitcast.14, bf16[128,256]{1,0:T(8,128)(2,1)} %constant.22.clone.tx_hbm, bf16[256,256]{1,0:T(8,128)(2,1)} %constant.23.clone.ty_hbm), custom_call_target="tpu_custom_call" | custom-call | flops 4000000000 | bytes 9000000 | tf_op jit(solution)/shard_map/forward_planes/pallas_call | solution.py:191
  7.3 12.7 %all-to-all-start = ((f32[64,16,128]{2,1,0:T(8,128)}), f32[64,16,128]{2,1,0:T(8,128)S(1)}, u32[]{:S(2)}, u32[]{:S(2)}) async-start(f32[64,16,128]{2,1,0:T(8,128)} %bitcast.12), calls=%async_computation | async-start | bytes 1048576 | tf_op jit(solution)/shard_map/all_to_all | solution.py:379
  20.0 0.0 copy-done.7
  20.0 0.1 copy.16.w_ref
  20.1 17.4 %all-to-all-done = f32[64,16,128]{2,1,0:T(8,128)S(1)} async-done(((f32[64,16,128]{2,1,0:T(8,128)}), f32[64,16,128]{2,1,0:T(8,128)S(1)}, u32[]{:S(2)}, u32[]{:S(2)}) %all-to-all-start) | async-done | bytes 524320 | tf_op jit(solution)/shard_map/all_to_all | solution.py:379
  37.5 0.0 copy-done
  37.5 0.0 copy-done.1
  37.5 0.0 copy-done.4
  37.5 0.0 copy-done.6
  37.6 0.0 copy-start.3
  37.6 0.0 copy-start.5
  37.6 2.3 %middle_modes.1 = (f32[512,128]{1,0:T(8,128)}, f32[24,512]{1,0:T(8,128)S(1)}) custom-call(f32[1024,128]{1,0:T(8,128)S(1)} %bitcast.9, bf16[2,16,17,256]{3,2,1,0:T(8,128)(2,1)S(1)} %copy.16.w_ref, bf16[48,384]{1,0:T(8,128)(2,1)S(1)} %copy-done, bf16[512,512]{1,0:T(8,128)(2,1)S(1)} %copy-done.1, bf16[512,512]{1,0:T(8,128)(2,1)S(1)} %copy-done.4, ...), custom_call_target="tpu_custom_call" | custom-call | flops 2000000000 | bytes 3000000 | tf_op jit(solution)/shard_map/middle_modes/pallas_call | solution.py:260
  39.9 6.1 %all-to-all-start.1 = ((f32[64,8,128]{2,1,0:T(8,128)}), f32[64,8,128]{2,1,0:T(8,128)S(1)}, u32[]{:S(2)}, u32[]{:S(2)}) async-start(f32[64,8,128]{2,1,0:T(8,128)} %bitcast.4), calls=%async_computation.1 | async-start | bytes 524288 | tf_op jit(solution)/shard_map/all_to_all | solution.py:379
  46.0 0.3 input_modes.1.a_ref
  46.3 0.1 collective-permute-start
  46.4 0.7 %collective-permute-start.1 = (f32[24,1024]{1,0:T(8,128)S(1)}, f32[24,1024]{1,0:T(8,128)S(1)}, u32[]{:S(2)}, u32[]{:S(2)}) collective-permute-start(f32[24,1024]{1,0:T(8,128)S(1)} %input_modes.1.a_ref), channel_id=1, source_target_pairs={{0,2},{1,3},{2,0},{3,1},{4,6},{5,7},{6,4},{7,5},{8,10},{9,11},{10,... | collective-permute-start | bytes 294920 | tf_op jit(solution)/shard_map/ppermute | solution.py:390
  47.1 2.7 %collective-permute-start.2 = (f32[24,1024]{1,0:T(8,128)S(1)}, f32[24,1024]{1,0:T(8,128)S(1)}, u32[]{:S(2)}, u32[]{:S(2)}) collective-permute-start(f32[24,1024]{1,0:T(8,128)S(1)} %input_modes.1.a_ref), channel_id=1, source_target_pairs={{0,3},{1,2},{2,1},{3,0},{4,7},{5,6},{6,5},{7,4},{8,11},{9,10},{10,... | collective-permute-start | bytes 294920 | tf_op jit(solution)/shard_map/ppermute | solution.py:390
  49.8 8.8 %all-to-all-done.1 = f32[64,8,128]{2,1,0:T(8,128)S(1)} async-done(((f32[64,8,128]{2,1,0:T(8,128)}), f32[64,8,128]{2,1,0:T(8,128)S(1)}, u32[]{:S(2)}, u32[]{:S(2)}) %all-to-all-start.1) | async-done | bytes 262176 | tf_op jit(solution)/shard_map/all_to_all | solution.py:379
  58.6 0.0 copy-done.3
  58.6 0.0 copy-done.5
  58.6 0.0 copy-start.2
  58.6 3.2 %back_planes.1 = bf16[8,4,256,256]{3,2,1,0:T(8,128)(2,1)} custom-call(f32[512,128]{1,0:T(8,128)S(1)} %bitcast.11, bf16[512,512]{1,0:T(8,128)(2,1)S(1)} %copy-done.3, bf16[256,192]{1,0:T(8,128)(2,1)S(1)} %copy-done.5), custom_call_target="tpu_custom_call" | custom-call | flops 4000000000 | bytes 6000000 | tf_op jit(solution)/shard_map/back_planes/pallas_call | solution.py:362
  61.8 0.0 collective-permute-done.b_ref
  61.8 0.0 collective-permute-done.1.c_ref
  61.8 0.0 collective-permute-done.2.d_ref
  61.8 0.0 copy-done.2
  61.8 1.7 %weight_terms.1 = f32[2,17,4,256]{3,2,1,0:T(4,128)} custom-call(s32[1]{0:T(128)} %bitcast.7.own_ref, f32[24,1024]{1,0:T(8,128)S(1)} %input_modes.1.a_ref, f32[24,1024]{1,0:T(8,128)S(1)} %collective-permute-done.b_ref, f32[24,1024]{1,0:T(8,128)S(1)} %collective-permute-done.1.c_ref, f32[24,1024]{1,0:T(8,128)S(1)} %collective-permute-done.2.d_ref, ...), custom_call_target="tpu_custom_call" | custom-call | flops 2000000000 | bytes 2000000 | tf_op jit(solution)/shard_map/weight_terms/pallas_call | solution.py:316
Async XLA Ops:
  0.6 19.4 %copy-start.7 = (bf16[2,16,17,256]{3,1,2,0:T(8,128)(2,1)S(1)}, bf16[2,16,17,256]{3,1,2,0:T(8,128)(2,1)}, u32[]{:S(2)}) copy-start(bf16[2,16,17,256]{3,1,2,0:T(8,128)(2,1)} %param.16) | copy-start | bytes 835588
  0.6 36.9 %copy-start = (bf16[48,384]{1,0:T(8,128)(2,1)S(1)}, bf16[48,384]{1,0:T(8,128)(2,1)}, u32[]{:S(2)}) copy-start(bf16[48,384]{1,0:T(8,128)(2,1)} %constant.24.clone.tz_ref) | copy-start | bytes 110596
  0.7 36.9 %copy-start.1 = (bf16[512,512]{1,0:T(8,128)(2,1)S(1)}, bf16[512,512]{1,0:T(8,128)(2,1)}, u32[]{:S(2)}) copy-start(bf16[512,512]{1,0:T(8,128)(2,1)} %constant.25.clone.e_ref.eg_ref) | copy-start | bytes 1572868
  0.7 36.9 %copy-start.4 = (bf16[512,512]{1,0:T(8,128)(2,1)S(1)}, bf16[512,512]{1,0:T(8,128)(2,1)}, u32[]{:S(2)}) copy-start(bf16[512,512]{1,0:T(8,128)(2,1)} %constant.26.clone.c_ref) | copy-start | bytes 1572868
  0.7 36.9 %copy-start.6 = (bf16[128,144]{1,0:T(8,128)(2,1)S(1)}, bf16[128,144]{1,0:T(8,128)(2,1)}, u32[]{:S(2)}) copy-start(bf16[128,144]{1,0:T(8,128)(2,1)} %constant.27.clone.tb_ref) | copy-start | bytes 110596
  7.3 30.2 %all-to-all-start = ((f32[64,16,128]{2,1,0:T(8,128)}), f32[64,16,128]{2,1,0:T(8,128)S(1)}, u32[]{:S(2)}, u32[]{:S(2)}) async-start(f32[64,16,128]{2,1,0:T(8,128)} %bitcast.12), calls=%async_computation | async-start | bytes 1048576 | tf_op jit(solution)/shard_map/all_to_all | solution.py:379
  37.6 21.0 %copy-start.3 = (bf16[512,512]{1,0:T(8,128)(2,1)S(1)}, bf16[512,512]{1,0:T(8,128)(2,1)}, u32[]{:S(2)}) copy-start(bf16[512,512]{1,0:T(8,128)(2,1)} %constant.28.clone.ty_ref) | copy-start | bytes 1572868
  37.6 21.0 %copy-start.5 = (bf16[256,192]{1,0:T(8,128)(2,1)S(1)}, bf16[256,192]{1,0:T(8,128)(2,1)}, u32[]{:S(2)}) copy-start(bf16[256,192]{1,0:T(8,128)(2,1)} %constant.29.clone.tx_ref) | copy-start | bytes 294916
  39.9 18.6 %all-to-all-start.1 = ((f32[64,8,128]{2,1,0:T(8,128)}), f32[64,8,128]{2,1,0:T(8,128)S(1)}, u32[]{:S(2)}, u32[]{:S(2)}) async-start(f32[64,8,128]{2,1,0:T(8,128)} %bitcast.4), calls=%async_computation.1 | async-start | bytes 524288 | tf_op jit(solution)/shard_map/all_to_all | solution.py:379
  46.3 15.5 %collective-permute-start = (f32[24,1024]{1,0:T(8,128)S(1)}, f32[24,1024]{1,0:T(8,128)S(1)}, u32[]{:S(2)}, u32[]{:S(2)}) collective-permute-start(f32[24,1024]{1,0:T(8,128)S(1)} %input_modes.1.a_ref), channel_id=1, source_target_pairs={{0,1},{1,0},{2,3},{3,2},{4,5},{5,4},{6,7},{7,6},{8,9},{9,8},{10,11... | collective-permute-start | bytes 294920 | tf_op jit(solution)/shard_map/ppermute | solution.py:390
  46.4 15.4 %collective-permute-start.1 = (f32[24,1024]{1,0:T(8,128)S(1)}, f32[24,1024]{1,0:T(8,128)S(1)}, u32[]{:S(2)}, u32[]{:S(2)}) collective-permute-start(f32[24,1024]{1,0:T(8,128)S(1)} %input_modes.1.a_ref), channel_id=1, source_target_pairs={{0,2},{1,3},{2,0},{3,1},{4,6},{5,7},{6,4},{7,5},{8,10},{9,11},{10,... | collective-permute-start | bytes 294920 | tf_op jit(solution)/shard_map/ppermute | solution.py:390
  47.1 14.7 %collective-permute-start.2 = (f32[24,1024]{1,0:T(8,128)S(1)}, f32[24,1024]{1,0:T(8,128)S(1)}, u32[]{:S(2)}, u32[]{:S(2)}) collective-permute-start(f32[24,1024]{1,0:T(8,128)S(1)} %input_modes.1.a_ref), channel_id=1, source_target_pairs={{0,3},{1,2},{2,1},{3,0},{4,7},{5,6},{6,5},{7,4},{8,11},{9,10},{10,... | collective-permute-start | bytes 294920 | tf_op jit(solution)/shard_map/ppermute | solution.py:390
  58.6 3.3 %copy-start.2 = (bf16[512,512]{1,0:T(8,128)(2,1)S(1)}, bf16[512,512]{1,0:T(8,128)(2,1)}, u32[]{:S(2)}) copy-start(bf16[512,512]{1,0:T(8,128)(2,1)} %constant.30.clone.eu_ref) | copy-start | bytes 1572868

commit v2 on v1

--- a/solution.py
+++ b/solution.py
@@ -84,22 +84,36 @@
     return np.concatenate([high, high, low], 1)
 
 
-def lane_fields():
-    lane = np.arange(512)
-    return lane // 128, lane // 64 % 2, lane // 16 % 4, lane % 16
-
-
-def expand_table(which):
-    cg, ri, c4, _ = lane_fields()
-    col = np.arange(512)
-    col_ri, ci, co = col // 256, col // 16 % 16, col % 16
-    target = ci if which == 0 else co
-    hit = (ri[:, None] == col_ri[None]) & ((cg * 4 + c4)[:, None] == target[None])
-    return hit.astype(ml_dtypes.bfloat16)
+def channel_mode_lanes():
+    lane = np.arange(256)
+    return lane // 16, lane % 16
+
+
+def expand_table():
+    c, _ = channel_mode_lanes()
+    col = np.arange(256)
+    return (c[:, None] == (col % 16)[None]).astype(ml_dtypes.bfloat16)
 
 
 def collect_table():
-    return np.ascontiguousarray(expand_table(0).T)
+    c, _ = channel_mode_lanes()
+    row = np.arange(256)
+    return ((row // 16)[:, None] == c[None]).astype(ml_dtypes.bfloat16)
+
+
+def quarter_table():
+    c, ky = channel_mode_lanes()
+    table = np.zeros((2, 256, 512), np.float32)
+    for part in range(2):
+        table[part, np.arange(256), ky // 4 * 128 + part * 64 + c * 4 + ky % 4] = 1.0
+    return table.reshape(512, 512).astype(ml_dtypes.bfloat16)
+
+
+def owned_table(which):
+    row, col = np.arange(128), np.arange(512)
+    target = col // 16 % 16 if which == 0 else col % 16
+    hit = (row // 64)[:, None] == (col // 256)[None]
+    return (hit & ((row // 4 % 16)[:, None] == target[None])).astype(ml_dtypes.bfloat16)
 
 
 def y_back_table():
@@ -210,45 +224,69 @@
     )
 
 
+def roll_half(value):
+    return pltpu.roll(value, 64, 1)
+
+
 def depth_modes(r_ref, first, tz_ref):
     tiles = []
     for cg in range(4):
         rows = [r_ref[pl.ds(first + p * 4 + cg, SLABS, stride=16), :] for p in range(2)]
         tiles.append(jnp.concatenate(rows, 0))
     high, low = split(jnp.concatenate(tiles, 1))
-    both = dot(tz_ref[...], jnp.concatenate([high, low, high], 0))
-    cos_part, sin_part = both[:KP], both[KP:]
-    sign = jnp.where(lane_iota(KP, 512) % 128 < 64, SCALE, -SCALE)
-    return cos_part * SCALE + sign * swap_parts(sin_part)
-
-
-def spread(values, masks, table):
-    rows = jnp.concatenate([jnp.where(mask, value, 0.0) for value, mask in zip(values, masks)], 0)
-    high, low = split(rows)
-    return dot(high, table) + dot(low, table)
-
-
-def middle_kernel(r_ref, w_ref, tz_ref, e_ref, c_ref, tb_ref, p_ref, g_ref, prod_ref):
-    modes = depth_modes(r_ref, 0, tz_ref)
-    g_ref[...] = modes
-    ky = lane_iota(KP, 512) % 16
-    masks = [ky == m for m in range(HALF)]
-    wide = spread([modes] * HALF, masks, e_ref[...])
-    prod_ref[...] = jnp.zeros_like(prod_ref)
-    for m in range(HALF):
-        row = m * KP
-        g_real, g_imag = wide[row:row + KZ, :256], wide[row:row + KZ, 256:]
-        w_real, w_imag = w_ref[0, m].astype(f32), w_ref[1, m].astype(f32)
-        prod_ref[row:row + KZ, :256] = g_real * w_real + g_imag * w_imag
-        prod_ref[row:row + KZ, 256:] = g_imag * w_real - g_real * w_imag
-    high, low = split(prod_ref[...])
-    sums = dot(high, c_ref[...]) + dot(low, c_ref[...])
-    direct = jnp.where(masks[0], sums[:KP], 0.0)
-    for m in range(1, HALF):
-        direct = direct + jnp.where(masks[m], sums[m * KP:(m + 1) * KP], 0.0)
-    sign = jnp.where(lane_iota(KP, 512) % 128 < 64, -1.0, 1.0)
-    turned = sign * swap_parts(direct)
-    high, low = split(jnp.concatenate([direct, turned], 0))
+    both = dot(tz_ref[...], jnp.concatenate([high, low, high], 0)) * SCALE
+    left = lane_iota(KP, 128) < 64
+    real, imag = [], []
+    for pair in range(2):
+        cuts = [slice((2 * pair + j) * 128, (2 * pair + j + 1) * 128) for j in range(2)]
+        c0, c1 = both[:KP, cuts[0]], both[:KP, cuts[1]]
+        s0, s1 = both[KP:, cuts[0]], both[KP:, cuts[1]]
+        real.append(jnp.where(left, c0 + roll_half(s0), roll_half(c1) + s1))
+        imag.append(jnp.where(left, roll_half(c0) - s0, c1 - roll_half(s1)))
+    return jnp.concatenate(real, 1), jnp.concatenate(imag, 1)
+
+
+def precise_dot(value, table):
+    high, low = split(value)
+    both = dot(jnp.concatenate([high, low], 0), table)
+    return both[:value.shape[0]] + both[value.shape[0]:]
+
+
+def middle_kernel(r_ref, w_ref, tz_ref, e_ref, c_ref, tb_ref, p_ref, g_ref, sum_ref):
+    g_real, g_imag = depth_modes(r_ref, 0, tz_ref)
+    g_ref[:KP] = g_real
+    g_ref[KP:] = g_imag
+    own = lane_iota(HALF, 256) % 16 == lax.broadcasted_iota(jnp.int32, (HALF, 256), 0)
+    rows = []
+    for part in range(2):
+        for kz in range(KZ):
+            line = g_ref[part * KP + kz:part * KP + kz + 1, :]
+            rows.append(jnp.where(own, jnp.broadcast_to(line, (HALF, 256)), 0.0))
+    wide = precise_dot(jnp.concatenate(rows, 0), e_ref[...])
+    real, imag = [], []
+    for kz in range(KZ):
+        g_r = wide[kz * HALF:(kz + 1) * HALF]
+        g_i = wide[(KZ + kz) * HALF:(KZ + kz + 1) * HALF]
+        w_r, w_i = w_ref[0, kz].astype(f32), w_ref[1, kz].astype(f32)
+        real.append(g_r * w_r + g_i * w_i)
+        imag.append(g_i * w_r - g_r * w_i)
+    sums = precise_dot(jnp.concatenate(real + imag, 0), c_ref[...])
+    sum_ref[...] = jnp.zeros_like(sum_ref)
+    for part in range(2):
+        for kz in range(KZ):
+            row = (part * KZ + kz) * HALF
+            kept = jnp.where(own, sums[row:row + HALF], 0.0)
+            sum_ref[part * KP + kz:part * KP + kz + 1, :] = jnp.sum(kept, axis=0, keepdims=True)
+    left = lane_iota(KP, 128) < 64
+    direct, turned = [], []
+    for pair in range(2):
+        cut = slice(pair * 128, (pair + 1) * 128)
+        re, im = sum_ref[:KP, cut], sum_ref[KP:, cut]
+        re_roll, im_roll = roll_half(re), roll_half(im)
+        direct.extend([jnp.where(left, re, im_roll), jnp.where(left, re_roll, im)])
+        turned.extend([jnp.where(left, -im, re_roll), jnp.where(left, -im_roll, re)])
+    stacked = jnp.concatenate([jnp.concatenate(direct, 1), jnp.concatenate(turned, 1)], 0)
+    high, low = split(stacked)
     planes = dot(tb_ref[...], jnp.concatenate([high, low, high], 0))
     for p in range(2):
         for cg in range(4):
@@ -261,67 +299,81 @@
         middle_kernel,
         out_shape=(
             jax.ShapeDtypeStruct((SLABS * 8, 128), f32),
-            jax.ShapeDtypeStruct((KP, 512), f32),
+            jax.ShapeDtypeStruct((2 * KP, 256), f32),
         ),
-        scratch_shapes=[pltpu.VMEM((HALF * KP, 512), f32)],
+        scratch_shapes=[pltpu.VMEM((2 * KP, 256), f32)],
         compiler_params=pltpu.CompilerParams(vmem_limit_bytes=VMEM_LIMIT),
         cost_estimate=pl.CostEstimate(flops=2 * 10**9, bytes_accessed=3 * 10**6, transcendentals=0),
         name="middle_modes",
     )(
         received,
-        weights,
+        weights.transpose(0, 2, 1, 3),
         jnp.asarray(depth_forward_table()),
-        jnp.asarray(expand_table(1)),
+        jnp.asarray(expand_table()),
         jnp.asarray(collect_table()),
         jnp.asarray(depth_back_table()),
     )
 
 
-def input_kernel(r_ref, tz_ref, g_ref, out_ref):
-    out_ref[:, :512] = depth_modes(r_ref, 8, tz_ref)
-    out_ref[:, 512:] = g_ref[...]
-
-
-def input_modes(received, grad):
+def input_kernel(index_ref, r_ref, tz_ref, g_ref, cut_ref, own_ref, first_ref, second_ref, third_ref, all_ref):
+    u_real, u_imag = depth_modes(r_ref, 8, tz_ref)
+    real = jnp.concatenate([u_real, g_ref[:KP]], 0)
+    imag = jnp.concatenate([u_imag, g_ref[KP:]], 0)
+    lanes = precise_dot(real, cut_ref[:256]) + precise_dot(imag, cut_ref[256:])
+    for owner in range(4):
+        for field in range(2):
+            piece = lanes[field * KP:(field + 1) * KP, owner * 128:(owner + 1) * 128]
+            all_ref[owner, :, field * 128:(field + 1) * 128] = piece
+    me = index_ref[0]
+    for k, ref in enumerate((own_ref, first_ref, second_ref, third_ref)):
+        ref[...] = all_ref[me ^ k]
+
+
+def input_modes(index, received, grad):
+    vmem = pl.BlockSpec(memory_space=pltpu.VMEM)
     return pl.pallas_call(
         input_kernel,
-        out_shape=jax.ShapeDtypeStruct((KP, 1024), f32),
+        out_shape=(jax.ShapeDtypeStruct((KP, 256), f32),) * 4,
+        in_specs=[pl.BlockSpec(memory_space=pltpu.SMEM)] + [vmem] * 4,
+        out_specs=(vmem,) * 4,
+        scratch_shapes=[pltpu.VMEM((4, KP, 256), f32)],
         compiler_params=pltpu.CompilerParams(vmem_limit_bytes=VMEM_LIMIT),
         cost_estimate=pl.CostEstimate(flops=10**8, bytes_accessed=10**6, transcendentals=0),
         name="input_modes",
-    )(received, jnp.asarray(depth_forward_table()), grad)
-
-
-def weight_kernel(own_ref, a_ref, b_ref, c_ref, d_ref, eu_ref, eg_ref, out_ref):
-    ky = lane_iota(KP, 512) % 16 - 4 * own_ref[0]
-    masks = [ky == m for m in range(4)]
-    refs = (a_ref, b_ref, c_ref, d_ref)
-    u_all = spread([r[:, :512] for r in refs for _ in range(4)], masks * 4, eu_ref[...])
-    g_all = spread([r[:, 512:] for r in refs for _ in range(4)], masks * 4, eg_ref[...])
-    for m in range(4):
-        real = jnp.zeros((KP, 256), f32)
-        imag = jnp.zeros((KP, 256), f32)
-        for k in range(4):
-            row = (k * 4 + m) * KP
-            u_real, u_imag = u_all[row:row + KP, :256], u_all[row:row + KP, 256:]
-            g_real, g_imag = g_all[row:row + KP, :256], g_all[row:row + KP, 256:]
-            real = real + (u_real * g_real + u_imag * g_imag)
-            imag = imag + (u_real * g_imag - u_imag * g_real)
-        out_ref[0, :, m, :] = real[:KZ]
-        out_ref[1, :, m, :] = imag[:KZ]
-
-
-def weight_terms(own, pieces):
-    vmem = pl.BlockSpec(memory_space=pltpu.VMEM)
+    )(index, received, jnp.asarray(depth_forward_table()), grad, jnp.asarray(quarter_table()))
+
+
+def weight_kernel(a_ref, b_ref, c_ref, d_ref, eu_ref, eg_ref, out_ref, u_ref, g_ref):
+    mode = lane_iota(KP, 128) % 4
+    for k, ref in enumerate((a_ref, b_ref, c_ref, d_ref)):
+        for m in range(4):
+            rows = pl.ds(k * 4 * KP + m, KP, stride=4)
+            u_ref[rows, :] = jnp.where(mode == m, ref[:, :128], 0.0)
+            g_ref[rows, :] = jnp.where(mode == m, ref[:, 128:], 0.0)
+    u_all = precise_dot(u_ref[...], eu_ref[...])
+    g_all = precise_dot(g_ref[...], eg_ref[...])
+    real = jnp.zeros((4 * KP, 256), f32)
+    imag = jnp.zeros((4 * KP, 256), f32)
+    for k in range(4):
+        cut = slice(k * 4 * KP, (k + 1) * 4 * KP)
+        u_r, u_i = u_all[cut, :256], u_all[cut, 256:]
+        g_r, g_i = g_all[cut, :256], g_all[cut, 256:]
+        real = real + (u_r * g_r + u_i * g_i)
+        imag = imag + (u_r * g_i - u_i * g_r)
+    for kz in range(KZ):
+        out_ref[0, kz] = real[kz * 4:(kz + 1) * 4]
+        out_ref[1, kz] = imag[kz * 4:(kz + 1) * 4]
+
+
+def weight_terms(pieces):
     terms = pl.pallas_call(
         weight_kernel,
         out_shape=jax.ShapeDtypeStruct((2, KZ, 4, C * C), f32),
-        in_specs=[pl.BlockSpec(memory_space=pltpu.SMEM)] + [vmem] * 6,
-        out_specs=vmem,
+        scratch_shapes=[pltpu.VMEM((16 * KP, 128), f32), pltpu.VMEM((16 * KP, 128), f32)],
         compiler_params=pltpu.CompilerParams(vmem_limit_bytes=VMEM_LIMIT),
         cost_estimate=pl.CostEstimate(flops=2 * 10**9, bytes_accessed=2 * 10**6, transcendentals=0),
         name="weight_terms",
-    )(own, *pieces, jnp.asarray(expand_table(0)), jnp.asarray(expand_table(1)))
+    )(*pieces, jnp.asarray(owned_table(0)), jnp.asarray(owned_table(1)))
     return terms.transpose(0, 2, 1, 3)
 
 
@@ -381,17 +433,15 @@
 
 
 def body(field_in, cotangent, weights):
+    index = lax.axis_index("group").astype(jnp.int32).reshape(1)
     received = exchange(forward(cotangent, field_in), 16)
     planes, grad = middle(received, weights)
     returned = exchange(planes, 8)
-    own = input_modes(received, grad)
-    pieces = [own]
+    pieces = list(input_modes(index, received, grad))
     for k in range(1, 4):
-        pieces.append(lax.ppermute(own, "group", [(i, i ^ k) for i in range(4)]))
-    index = lax.axis_index("group").astype(jnp.int32).reshape(1)
-    field_grad = back(returned)
-    pieces, field_grad = lax.optimization_barrier((pieces, field_grad))
-    return (field_grad, weight_terms(index, pieces))
+        pieces[k] = lax.ppermute(pieces[k], "group", [(i, i ^ k) for i in range(4)])
+    weight_grad = weight_terms(pieces)
+    return (back(returned), weight_grad)
 
 
 def solution(mesh):

time: 63.8 us -> 61.7 us (0.967)
  blocking collectives: 0 us -> 30.2 us
  waiting for transfers between devices: 26.2 us -> 7.3 us
  starting transfers between devices: 22.2 us -> 9.52 us
    all_to_all x0 -> x1, blocking collectives: none -> 30.2 us  [exchange(): lax.all_to_all(chunks.reshape(SLABS, rows, 128), 'slab', 0, 0, tiled=True)]
    all_to_all x2 -> x1, waiting for transfers between devices: 26.2 us -> 4.5 us  [exchange(): lax.all_to_all(chunks.reshape(SLABS, rows, 128), 'slab', 0, 0, tiled=True)]
    all_to_all x2 -> x1, starting transfers between devices: 18.7 us -> 6.06 us  [exchange(): lax.all_to_all(chunks.reshape(SLABS, rows, 128), 'slab', 0, 0, tiled=True)]
    ppermute x3, waiting for transfers between devices: 0.01 us -> 2.8 us  [body(): pieces[k] = lax.ppermute(pieces[k], 'group', [(i, i ^ k) for i in range(4)])]
  transfers between devices with their start and end apart: 5 -> 4, of which waited for: 2 -> 3; matrix products, arithmetic and copies ran while one was open for 0% -> 0% of each run, Pallas kernels for 6% -> 3%
where the time goes in v2:
time: 61.7 us; the launch traced here: 61.5 us
  blocking collectives  30.2 us (49%)
  Pallas kernels  13.6 us (22%)
  starting transfers between devices  9.52 us (15%)
  waiting for transfers between devices  7.3 us (12%)
  between operations  0.77 us (1%)
    all_to_all x1, blocking collectives, exchange(): lax.all_to_all(chunks.reshape(SLABS, rows, 128), 'slab', 0, 0, tiled=True)  30.2 us
    pallas_call x1, Pallas kernels, forward(): pl.pallas_call(forward_kernel, out_shape=jax.ShapeDtypeStruct((SLABS * 16...  6.57 us
    all_to_all x1, starting transfers between devices, exchange(): lax.all_to_all(chunks.reshape(SLABS, rows, 128), 'slab', 0, 0, tiled=True)  6.06 us
    all_to_all x1, waiting for transfers between devices, exchange(): lax.all_to_all(chunks.reshape(SLABS, rows, 128), 'slab', 0, 0, tiled=True)  4.5 us
    ppermute x3, starting transfers between devices, body(): pieces[k] = lax.ppermute(pieces[k], 'group', [(i, i ^ k) for i in range(4)])  3.46 us
    pallas_call x1, Pallas kernels, back(): pl.pallas_call(back_kernel, out_shape=jax.ShapeDtypeStruct((8, 4, NX, NY)...  3.23 us
    ppermute x3, waiting for transfers between devices, body(): pieces[k] = lax.ppermute(pieces[k], 'group', [(i, i ^ k) for i in range(4)])  2.8 us
    pallas_call x1, Pallas kernels, middle(): pl.pallas_call(middle_kernel, out_shape=(jax.ShapeDtypeStruct((SLABS * 8,...  2.08 us
  transfers between devices with their start and end apart: 4, of which 3 were waited for; matrix products, arithmetic and copies ran while one was open for 0% of the time, Pallas kernels for 3%

profile of v2, /device:TPU:16, one launch (start us, length us, event | category | flops | bytes accessed | tf_op | source)
XLA Modules:
  0.0 61.5 jit_solution(11132403079446754818)
XLA Ops:
  0.6 0.0 copy-start.1
  0.6 0.0 copy-start.2
  0.7 0.0 copy-start.7
  0.7 0.0 copy-start.8
  0.7 0.0 copy-start.9
  0.7 6.6 %forward_planes.1 = f32[1024,128]{1,0:T(8,128)} custom-call(bf16[32,256,256]{2,1,0:T(8,128)(2,1)} %bitcast.15, bf16[32,256,256]{2,1,0:T(8,128)(2,1)} %bitcast.16, bf16[128,256]{1,0:T(8,128)(2,1)} %constant.26.clone.tx_hbm, bf16[256,256]{1,0:T(8,128)(2,1)} %constant.27.clone.ty_hbm), custom_call_target="tpu_custom_call" | custom-call | flops 4000000000 | bytes 9000000 | tf_op jit(solution)/shard_map/forward_planes/pallas_call | solution.py:205
  7.3 30.2 %all_to_all.10 = f32[64,16,128]{2,1,0:T(8,128)S(1)} all-to-all(f32[64,16,128]{2,1,0:T(8,128)} %bitcast.14), channel_id=1, replica_groups=mesh['slab'=64,'group'=4] {'slab'}, dimensions={0} | all-to-all | bytes 1048576 | tf_op jit(solution)/shard_map/all_to_all | solution.py:431
  37.5 0.0 copy-start
  37.5 0.0 copy-done.1
  37.5 0.0 copy-done.2
  37.5 0.0 copy-done.7
  37.5 0.0 copy-done.8
  37.5 0.0 copy-done.9
  37.5 0.0 copy-start.5
  37.5 0.0 copy-start.6
  37.5 2.1 %middle_modes.1 = (f32[512,128]{1,0:T(8,128)}, f32[48,256]{1,0:T(8,128)S(1)}) custom-call(f32[1024,128]{1,0:T(8,128)S(1)} %bitcast.10, bf16[2,17,16,256]{3,2,1,0:T(8,128)(2,1)S(1)} %bitcast.13, bf16[48,384]{1,0:T(8,128)(2,1)S(1)} %copy-done.1, bf16[256,256]{1,0:T(8,128)(2,1)S(1)} %copy-done.8, bf16[256,256]{1,0:T(8,128)(2,1)S(1)} %copy-done.7, ...), custom_call_target="tpu_custom_call" | custom-call | flops 2000000000 | bytes 3000000 | tf_op jit(solution)/shard_map/middle_modes/pallas_call | solution.py:298
  39.6 6.1 %all-to-all-start.1 = ((f32[64,8,128]{2,1,0:T(8,128)}), f32[64,8,128]{2,1,0:T(8,128)S(1)}, u32[]{:S(2)}, u32[]{:S(2)}) async-start(f32[64,8,128]{2,1,0:T(8,128)} %bitcast.5), calls=%async_computation.1 | async-start | bytes 524288 | tf_op jit(solution)/shard_map/all_to_all | solution.py:431
  45.7 0.0 copy-done
  45.7 0.0 copy-start.3
  45.7 0.0 copy-start.4
  45.7 0.5 input_modes.1
  46.3 0.1 collective-permute-start
  46.4 0.7 %collective-permute-start.1 = (f32[24,256]{1,0:T(8,128)S(1)}, f32[24,256]{1,0:T(8,128)S(1)}, u32[]{:S(2)}, u32[]{:S(2)}) collective-permute-start(f32[24,256]{1,0:T(8,128)S(1)} %get-tuple-element.12), channel_id=1, source_target_pairs={{0,2},{1,3},{2,0},{3,1},{4,6},{5,7},{6,4},{7,5},{8,10},{9,11},{10,... | collective-permute-start | bytes 73736 | tf_op jit(solution)/shard_map/ppermute | solution.py:442
  47.1 2.7 %collective-permute-start.2 = (f32[24,256]{1,0:T(8,128)S(1)}, f32[24,256]{1,0:T(8,128)S(1)}, u32[]{:S(2)}, u32[]{:S(2)}) collective-permute-start(f32[24,256]{1,0:T(8,128)S(1)} %get-tuple-element.13), channel_id=1, source_target_pairs={{0,3},{1,2},{2,1},{3,0},{4,7},{5,6},{6,5},{7,4},{8,11},{9,10},{10,... | collective-permute-start | bytes 73736 | tf_op jit(solution)/shard_map/ppermute | solution.py:442
  49.7 0.0 collective-permute-done.b_ref
  49.7 2.7 %collective-permute-done.1.c_ref = f32[24,256]{1,0:T(8,128)S(1)} collective-permute-done((f32[24,256]{1,0:T(8,128)S(1)}, f32[24,256]{1,0:T(8,128)S(1)}, u32[]{:S(2)}, u32[]{:S(2)}) %collective-permute-start.1) | collective-permute-done | bytes 24608 | tf_op jit(solution)/shard_map/ppermute | solution.py:442
  52.4 0.1 collective-permute-done.2.d_ref
  52.5 0.0 copy-done.5
  52.5 0.0 copy-done.6
  52.5 1.2 %weight_terms.1 = f32[2,17,4,256]{3,2,1,0:T(4,128)} custom-call(f32[24,256]{1,0:T(8,128)S(1)} %get-tuple-element.10.a_ref, f32[24,256]{1,0:T(8,128)S(1)} %collective-permute-done.b_ref, f32[24,256]{1,0:T(8,128)S(1)} %collective-permute-done.1.c_ref, f32[24,256]{1,0:T(8,128)S(1)} %collective-permute-done.2.d_ref, bf16[128,512]{1,0:T(8,128)(2,1)S(1)} %copy-done.6, ...), custom_call_target="tpu_custom_call" | custom-call | flops 2000000000 | bytes 2000000 | tf_op jit(solution)/shard_map/weight_terms/pallas_call | solution.py:369
  53.8 4.5 %all-to-all-done.1 = f32[64,8,128]{2,1,0:T(8,128)S(1)} async-done(((f32[64,8,128]{2,1,0:T(8,128)}), f32[64,8,128]{2,1,0:T(8,128)S(1)}, u32[]{:S(2)}, u32[]{:S(2)}) %all-to-all-start.1) | async-done | bytes 262176 | tf_op jit(solution)/shard_map/all_to_all | solution.py:431
  58.3 0.0 copy-done.3
  58.3 0.0 copy-done.4
  58.3 3.2 %back_planes.1 = bf16[8,4,256,256]{3,2,1,0:T(8,128)(2,1)} custom-call(f32[512,128]{1,0:T(8,128)S(1)} %bitcast.12, bf16[512,512]{1,0:T(8,128)(2,1)S(1)} %copy-done.3, bf16[256,192]{1,0:T(8,128)(2,1)S(1)} %copy-done.4), custom_call_target="tpu_custom_call" | custom-call | flops 4000000000 | bytes 6000000 | tf_op jit(solution)/shard_map/back_planes/pallas_call | solution.py:414
Async XLA Ops:
  0.6 36.9 %copy-start.1 = (bf16[48,384]{1,0:T(8,128)(2,1)S(1)}, bf16[48,384]{1,0:T(8,128)(2,1)}, u32[]{:S(2)}) copy-start(bf16[48,384]{1,0:T(8,128)(2,1)} %constant.28.clone.tz_ref) | copy-start | bytes 110596
  0.6 36.8 %copy-start.2 = (bf16[2,16,17,256]{3,1,2,0:T(8,128)(2,1)S(1)}, bf16[2,16,17,256]{3,1,2,0:T(8,128)(2,1)}, u32[]{:S(2)}) copy-start(bf16[2,16,17,256]{3,1,2,0:T(8,128)(2,1)} %param.17) | copy-start | bytes 835588
  0.7 36.8 %copy-start.7 = (bf16[256,256]{1,0:T(8,128)(2,1)S(1)}, bf16[256,256]{1,0:T(8,128)(2,1)}, u32[]{:S(2)}) copy-start(bf16[256,256]{1,0:T(8,128)(2,1)} %constant.30.clone.c_ref) | copy-start | bytes 393220
  0.7 36.8 %copy-start.8 = (bf16[256,256]{1,0:T(8,128)(2,1)S(1)}, bf16[256,256]{1,0:T(8,128)(2,1)}, u32[]{:S(2)}) copy-start(bf16[256,256]{1,0:T(8,128)(2,1)} %constant.29.clone.e_ref) | copy-start | bytes 393220
  0.7 36.8 %copy-start.9 = (bf16[128,144]{1,0:T(8,128)(2,1)S(1)}, bf16[128,144]{1,0:T(8,128)(2,1)}, u32[]{:S(2)}) copy-start(bf16[128,144]{1,0:T(8,128)(2,1)} %constant.31.clone.tb_ref) | copy-start | bytes 110596
  37.5 8.2 %copy-start = (bf16[512,512]{1,0:T(8,128)(2,1)S(1)}, bf16[512,512]{1,0:T(8,128)(2,1)}, u32[]{:S(2)}) copy-start(bf16[512,512]{1,0:T(8,128)(2,1)} %constant.32.clone.cut_ref) | copy-start | bytes 1572868
  37.5 15.0 %copy-start.5 = (bf16[128,512]{1,0:T(8,128)(2,1)S(1)}, bf16[128,512]{1,0:T(8,128)(2,1)}, u32[]{:S(2)}) copy-start(bf16[128,512]{1,0:T(8,128)(2,1)} %constant.34.clone.eg_ref) | copy-start | bytes 393220
  37.5 15.0 %copy-start.6 = (bf16[128,512]{1,0:T(8,128)(2,1)S(1)}, bf16[128,512]{1,0:T(8,128)(2,1)}, u32[]{:S(2)}) copy-start(bf16[128,512]{1,0:T(8,128)(2,1)} %constant.33.clone.eu_ref) | copy-start | bytes 393220
  39.6 18.6 %all-to-all-start.1 = ((f32[64,8,128]{2,1,0:T(8,128)}), f32[64,8,128]{2,1,0:T(8,128)S(1)}, u32[]{:S(2)}, u32[]{:S(2)}) async-start(f32[64,8,128]{2,1,0:T(8,128)} %bitcast.5), calls=%async_computation.1 | async-start | bytes 524288 | tf_op jit(solution)/shard_map/all_to_all | solution.py:431
  45.7 12.6 %copy-start.3 = (bf16[512,512]{1,0:T(8,128)(2,1)S(1)}, bf16[512,512]{1,0:T(8,128)(2,1)}, u32[]{:S(2)}) copy-start(bf16[512,512]{1,0:T(8,128)(2,1)} %constant.35.clone.ty_ref) | copy-start | bytes 1572868
  45.7 12.5 %copy-start.4 = (bf16[256,192]{1,0:T(8,128)(2,1)S(1)}, bf16[256,192]{1,0:T(8,128)(2,1)}, u32[]{:S(2)}) copy-start(bf16[256,192]{1,0:T(8,128)(2,1)} %constant.36.clone.tx_ref) | copy-start | bytes 294916
  46.3 3.5 %collective-permute-start = (f32[24,256]{1,0:T(8,128)S(1)}, f32[24,256]{1,0:T(8,128)S(1)}, u32[]{:S(2)}, u32[]{:S(2)}) collective-permute-start(f32[24,256]{1,0:T(8,128)S(1)} %get-tuple-element.11), channel_id=1, source_target_pairs={{0,1},{1,0},{2,3},{3,2},{4,5},{5,4},{6,7},{7,6},{8,9},{9,8},{10,11... | collective-permute-start | bytes 73736 | tf_op jit(solution)/shard_map/ppermute | solution.py:442
  46.4 6.1 %collective-permute-start.1 = (f32[24,256]{1,0:T(8,128)S(1)}, f32[24,256]{1,0:T(8,128)S(1)}, u32[]{:S(2)}, u32[]{:S(2)}) collective-permute-start(f32[24,256]{1,0:T(8,128)S(1)} %get-tuple-element.12), channel_id=1, source_target_pairs={{0,2},{1,3},{2,0},{3,1},{4,6},{5,7},{6,4},{7,5},{8,10},{9,11},{10,... | collective-permute-start | bytes 73736 | tf_op jit(solution)/shard_map/ppermute | solution.py:442
  47.1 5.5 %collective-permute-start.2 = (f32[24,256]{1,0:T(8,128)S(1)}, f32[24,256]{1,0:T(8,128)S(1)}, u32[]{:S(2)}, u32[]{:S(2)}) collective-permute-start(f32[24,256]{1,0:T(8,128)S(1)} %get-tuple-element.13), channel_id=1, source_target_pairs={{0,3},{1,2},{2,1},{3,0},{4,7},{5,6},{6,5},{7,4},{8,11},{9,10},{10,... | collective-permute-start | bytes 73736 | tf_op jit(solution)/shard_map/ppermute | solution.py:442

commit v3 on v2

--- a/solution.py
+++ b/solution.py
@@ -96,9 +96,10 @@
 
 
 def collect_table():
-    c, _ = channel_mode_lanes()
-    row = np.arange(256)
-    return ((row // 16)[:, None] == c[None]).astype(ml_dtypes.bfloat16)
+    row, col = np.arange(512), np.arange(512)
+    channel = col // 128 * 4 + col // 32 % 4
+    hit = (row // 256)[:, None] == (col // 16 % 2)[None]
+    return (hit & ((row // 16 % 16)[:, None] == channel[None])).astype(ml_dtypes.bfloat16)
 
 
 def quarter_table():
@@ -122,10 +123,10 @@
     rows = []
     for half in range(2):
         cut = slice(half * HALF, (half + 1) * HALF)
-        rows.extend([np.concatenate([cos[cut], sin[cut]], 1)] * 4)
-        rows.extend([np.concatenate([-sin[cut], cos[cut]], 1)] * 4)
+        rows.append(np.concatenate([cos[cut], sin[cut]], 1))
+        rows.append(np.concatenate([-sin[cut], cos[cut]], 1))
     high, low = split_np(np.concatenate(rows, 0))
-    return np.concatenate([high, low], 0)
+    return np.concatenate([high, high, low, np.zeros_like(low)], 0)
 
 
 def x_back_table():
@@ -204,7 +205,7 @@
     anywhere = pl.BlockSpec(memory_space=pl.ANY)
     return pl.pallas_call(
         forward_kernel,
-        out_shape=jax.ShapeDtypeStruct((SLABS * 16, 128), f32),
+        out_shape=pltpu.VMEM((SLABS * 16, 128), f32),
         in_specs=[anywhere] * 4,
         scratch_shapes=[
             pltpu.VMEM((STEPS * 4, NX, NY), bf16),
@@ -263,29 +264,25 @@
             line = g_ref[part * KP + kz:part * KP + kz + 1, :]
             rows.append(jnp.where(own, jnp.broadcast_to(line, (HALF, 256)), 0.0))
     wide = precise_dot(jnp.concatenate(rows, 0), e_ref[...])
-    real, imag = [], []
+    products = []
     for kz in range(KZ):
         g_r = wide[kz * HALF:(kz + 1) * HALF]
         g_i = wide[(KZ + kz) * HALF:(KZ + kz + 1) * HALF]
         w_r, w_i = w_ref[0, kz].astype(f32), w_ref[1, kz].astype(f32)
-        real.append(g_r * w_r + g_i * w_i)
-        imag.append(g_i * w_r - g_r * w_i)
-    sums = precise_dot(jnp.concatenate(real + imag, 0), c_ref[...])
+        products.append(jnp.concatenate([g_r * w_r + g_i * w_i, g_i * w_r - g_r * w_i], 1))
+    sums = precise_dot(jnp.concatenate(products, 0), c_ref[...])
+    own = jnp.concatenate([own, own], 1)
     sum_ref[...] = jnp.zeros_like(sum_ref)
-    for part in range(2):
-        for kz in range(KZ):
-            row = (part * KZ + kz) * HALF
-            kept = jnp.where(own, sums[row:row + HALF], 0.0)
-            sum_ref[part * KP + kz:part * KP + kz + 1, :] = jnp.sum(kept, axis=0, keepdims=True)
-    left = lane_iota(KP, 128) < 64
-    direct, turned = [], []
-    for pair in range(2):
-        cut = slice(pair * 128, (pair + 1) * 128)
-        re, im = sum_ref[:KP, cut], sum_ref[KP:, cut]
-        re_roll, im_roll = roll_half(re), roll_half(im)
-        direct.extend([jnp.where(left, re, im_roll), jnp.where(left, re_roll, im)])
-        turned.extend([jnp.where(left, -im, re_roll), jnp.where(left, -im_roll, re)])
-    stacked = jnp.concatenate([jnp.concatenate(direct, 1), jnp.concatenate(turned, 1)], 0)
+    for kz in range(KZ):
+        kept = jnp.where(own, sums[kz * HALF:(kz + 1) * HALF], 0.0)
+        sum_ref[kz:kz + 1, :] = jnp.sum(kept, axis=0, keepdims=True)
+    direct = sum_ref[...]
+    real_lane = lane_iota(KP, 128) % 32 < 16
+    turned = []
+    for cg in range(4):
+        tile = direct[:, cg * 128:(cg + 1) * 128]
+        turned.append(jnp.where(real_lane, -pltpu.roll(tile, 112, 1), pltpu.roll(tile, 16, 1)))
+    stacked = jnp.concatenate([direct, jnp.concatenate(turned, 1)], 0)
     high, low = split(stacked)
     planes = dot(tb_ref[...], jnp.concatenate([high, low, high], 0))
     for p in range(2):
@@ -297,11 +294,8 @@
 def middle(received, weights):
     return pl.pallas_call(
         middle_kernel,
-        out_shape=(
-            jax.ShapeDtypeStruct((SLABS * 8, 128), f32),
-            jax.ShapeDtypeStruct((2 * KP, 256), f32),
-        ),
-        scratch_shapes=[pltpu.VMEM((2 * KP, 256), f32)],
+        out_shape=pltpu.VMEM((SLABS * 8, 128), f32),
+        scratch_shapes=[pltpu.VMEM((2 * KP, 256), f32), pltpu.VMEM((KP, 512), f32)],
         compiler_params=pltpu.CompilerParams(vmem_limit_bytes=VMEM_LIMIT),
         cost_estimate=pl.CostEstimate(flops=2 * 10**9, bytes_accessed=3 * 10**6, transcendentals=0),
         name="middle_modes",
@@ -315,10 +309,11 @@
     )
 
 
-def input_kernel(index_ref, r_ref, tz_ref, g_ref, cut_ref, own_ref, first_ref, second_ref, third_ref, all_ref):
+def input_kernel(index_ref, r_ref, tz_ref, cut_ref, own_ref, first_ref, second_ref, third_ref, all_ref):
     u_real, u_imag = depth_modes(r_ref, 8, tz_ref)
-    real = jnp.concatenate([u_real, g_ref[:KP]], 0)
-    imag = jnp.concatenate([u_imag, g_ref[KP:]], 0)
+    g_real, g_imag = depth_modes(r_ref, 0, tz_ref)
+    real = jnp.concatenate([u_real, g_real], 0)
+    imag = jnp.concatenate([u_imag, g_imag], 0)
     lanes = precise_dot(real, cut_ref[:256]) + precise_dot(imag, cut_ref[256:])
     for owner in range(4):
         for field in range(2):
@@ -329,18 +324,18 @@
         ref[...] = all_ref[me ^ k]
 
 
-def input_modes(index, received, grad):
+def input_modes(index, received):
     vmem = pl.BlockSpec(memory_space=pltpu.VMEM)
     return pl.pallas_call(
         input_kernel,
         out_shape=(jax.ShapeDtypeStruct((KP, 256), f32),) * 4,
-        in_specs=[pl.BlockSpec(memory_space=pltpu.SMEM)] + [vmem] * 4,
+        in_specs=[pl.BlockSpec(memory_space=pltpu.SMEM)] + [vmem] * 3,
         out_specs=(vmem,) * 4,
         scratch_shapes=[pltpu.VMEM((4, KP, 256), f32)],
         compiler_params=pltpu.CompilerParams(vmem_limit_bytes=VMEM_LIMIT),
         cost_estimate=pl.CostEstimate(flops=10**8, bytes_accessed=10**6, transcendentals=0),
         name="input_modes",
-    )(index, received, jnp.asarray(depth_forward_table()), grad, jnp.asarray(quarter_table()))
+    )(index, received, jnp.asarray(depth_forward_table()), jnp.asarray(quarter_table()))
 
 
 def weight_kernel(a_ref, b_ref, c_ref, d_ref, eu_ref, eg_ref, out_ref, u_ref, g_ref):
@@ -366,42 +361,44 @@
 
 
 def weight_terms(pieces):
-    terms = pl.pallas_call(
+    return pl.pallas_call(
         weight_kernel,
-        out_shape=jax.ShapeDtypeStruct((2, KZ, 4, C * C), f32),
+        out_shape=pltpu.VMEM((2, KZ, 4, C * C), f32),
         scratch_shapes=[pltpu.VMEM((16 * KP, 128), f32), pltpu.VMEM((16 * KP, 128), f32)],
         compiler_params=pltpu.CompilerParams(vmem_limit_bytes=VMEM_LIMIT),
         cost_estimate=pl.CostEstimate(flops=2 * 10**9, bytes_accessed=2 * 10**6, transcendentals=0),
         name="weight_terms",
     )(*pieces, jnp.asarray(owned_table(0)), jnp.asarray(owned_table(1)))
-    return terms.transpose(0, 2, 1, 3)
-
-
-def back_kernel(r_ref, ty_ref, tx_ref, out_hbm, field_ref, q_ref, sems):
-    rows = []
-    for pg in range(8):
-        halves = [r_ref[pl.ds(half * 8 + pg, KX, stride=16), :] for half in range(2)]
-        rows.append(jnp.concatenate(halves, 1))
-    grid = jnp.concatenate(rows, 0)
-    slot = lane_iota(256, 256) // 16 % 4
+
+
+def back_kernel(r_ref, ty_ref, tx_ref, terms_ref, out_hbm, terms_hbm, field_ref, q_ref, sems):
+    copies = [pltpu.make_async_copy(terms_ref, terms_hbm, sems.at[32])]
+    copies[0].start()
+    highs, lows = [], []
+    for half in range(2):
+        rows = [r_ref[pl.ds(half * 8 + pg, KX, stride=16), :] for pg in range(8)]
+        grid = jnp.concatenate(rows, 0)
+        highs.append(grid.astype(bf16).astype(f32))
+        lows.append(grid - highs[-1])
+    parts = highs + lows
+    place = lane_iota(256, 128) // 32
 
     def rows_x(c4):
-        high, low = split(jnp.where(slot == c4, grid, 0.0))
-        mixed = dot(jnp.concatenate([high, low], 0), ty_ref[:256])
-        mixed = mixed[:256] + mixed[256:] + dot(high, ty_ref[256:])
-        high, low = split(mixed)
+        moved = [parts[t] if t == c4 else pltpu.roll(parts[t], (t - c4) % 4 * 32, 1) for t in range(4)]
+        lanes = jnp.where(place == 0, moved[0], jnp.where(place == 1, moved[1], jnp.where(place == 2, moved[2], moved[3])))
+        lanes = lanes.astype(bf16)
+        high, low = split(dot(jnp.concatenate([lanes, lanes], 1), ty_ref[...]))
         for pg in range(8):
             for part in range(2):
                 cut = (slice(pg * 32, (pg + 1) * 32), slice(part * 256, (part + 1) * 256))
                 q_ref[c4, pg, part * 32:(part + 1) * 32, :] = high[cut]
                 q_ref[c4, pg, 64 + part * 32:64 + (part + 1) * 32, :] = low[cut]
 
-    copies = []
     rows_x(0)
     for c4 in range(4):
-        if c4 < 3:
-            rows_x(c4 + 1)
         for pg in range(8):
+            if pg == 1 and c4 < 3:
+                rows_x(c4 + 1)
             q = q_ref[c4, pg]
             field_ref[pg, c4] = dot(tx_ref[...], jnp.concatenate([q, q[:64]], 0)).astype(bf16)
             copies.append(pltpu.make_async_copy(field_ref.at[pg, c4], out_hbm.at[pg, c4], sems.at[c4 * 8 + pg]))
@@ -410,21 +407,27 @@
         copy.wait()
 
 
-def back(received):
-    field = pl.pallas_call(
+def back(received, terms):
+    vmem = pl.BlockSpec(memory_space=pltpu.VMEM)
+    anywhere = pl.BlockSpec(memory_space=pl.ANY)
+    field, terms = pl.pallas_call(
         back_kernel,
-        out_shape=jax.ShapeDtypeStruct((8, 4, NX, NY), bf16),
-        out_specs=pl.BlockSpec(memory_space=pl.ANY),
+        out_shape=(
+            jax.ShapeDtypeStruct((8, 4, NX, NY), bf16),
+            jax.ShapeDtypeStruct((2, KZ, 4, C * C), f32),
+        ),
+        in_specs=[vmem] * 4,
+        out_specs=(anywhere, anywhere),
         scratch_shapes=[
             pltpu.VMEM((8, 4, NX, NY), bf16),
             pltpu.VMEM((4, 8, 128, NY), bf16),
-            pltpu.SemaphoreType.DMA((32,)),
+            pltpu.SemaphoreType.DMA((33,)),
         ],
         compiler_params=pltpu.CompilerParams(vmem_limit_bytes=VMEM_LIMIT),
         cost_estimate=pl.CostEstimate(flops=4 * 10**9, bytes_accessed=6 * 10**6, transcendentals=0),
         name="back_planes",
-    )(received, jnp.asarray(y_back_table()), jnp.asarray(x_back_table()))
-    return field.reshape(1, 2, C, NX, NY)
+    )(received, jnp.asarray(y_back_table()), jnp.asarray(x_back_table()), terms)
+    return field.reshape(1, 2, C, NX, NY), terms.transpose(0, 2, 1, 3)
 
 
 def exchange(chunks, rows):
@@ -435,13 +438,11 @@
 def body(field_in, cotangent, weights):
     index = lax.axis_index("group").astype(jnp.int32).reshape(1)
     received = exchange(forward(cotangent, field_in), 16)
-    planes, grad = middle(received, weights)
-    returned = exchange(planes, 8)
-    pieces = list(input_modes(index, received, grad))
+    returned = exchange(middle(received, weights), 8)
+    pieces = list(input_modes(index, received))
     for k in range(1, 4):
         pieces[k] = lax.ppermute(pieces[k], "group", [(i, i ^ k) for i in range(4)])
-    weight_grad = weight_terms(pieces)
-    return (back(returned), weight_grad)
+    return back(returned, weight_terms(pieces))
 
 
 def solution(mesh):

time: 61.7 us -> 60.3 us (0.977)
  Pallas kernels: 13.6 us -> 11.9 us
    pallas_call x4, Pallas kernels: 13.1 us -> 11.3 us  [the longest x1 5.77 us: forward(): pl.pallas_call(forward_kernel, out_shape=pltpu.VMEM((SLABS * 16, 128), f3...]
  transfers between devices with their start and end apart: 4 -> 4, of which waited for: 3 -> 3; matrix products, arithmetic and copies ran while one was open for 0% -> 0% of each run, Pallas kernels for 3% -> 2%
where the time goes in v3:
time: 60.3 us; the launch traced here: 60.1 us
  blocking collectives  30 us (50%)
  Pallas kernels  11.9 us (20%)
  starting transfers between devices  9.52 us (16%)
  waiting for transfers between devices  7.85 us (13%)
  between operations  0.78 us (1%)
    all_to_all x1, blocking collectives, exchange(): lax.all_to_all(chunks.reshape(SLABS, rows, 128), 'slab', 0, 0, tiled=True)  30 us
    all_to_all x1, starting transfers between devices, exchange(): lax.all_to_all(chunks.reshape(SLABS, rows, 128), 'slab', 0, 0, tiled=True)  6.06 us
    pallas_call x1, Pallas kernels, forward(): pl.pallas_call(forward_kernel, out_shape=pltpu.VMEM((SLABS * 16, 128), f3...  5.77 us
    all_to_all x1, waiting for transfers between devices, exchange(): lax.all_to_all(chunks.reshape(SLABS, rows, 128), 'slab', 0, 0, tiled=True)  5.01 us
    ppermute x3, starting transfers between devices, body(): pieces[k] = lax.ppermute(pieces[k], 'group', [(i, i ^ k) for i in range(4)])  3.46 us
    ppermute x3, waiting for transfers between devices, body(): pieces[k] = lax.ppermute(pieces[k], 'group', [(i, i ^ k) for i in range(4)])  2.85 us
    pallas_call x1, Pallas kernels, back(): pl.pallas_call(back_kernel, out_shape=(jax.ShapeDtypeStruct((8, 4, NX, NY...  2.83 us
    pallas_call x1, Pallas kernels, middle(): pl.pallas_call(middle_kernel, out_shape=pltpu.VMEM((SLABS * 8, 128), f32)...  2.1 us
  transfers between devices with their start and end apart: 4, of which 3 were waited for; matrix products, arithmetic and copies ran while one was open for 0% of the time, Pallas kernels for 2%

profile of v3, /device:TPU:16, one launch (start us, length us, event | category | flops | bytes accessed | tf_op | source)
XLA Modules:
  0.0 60.1 jit_solution(14823073296486722075)
XLA Ops:
  0.6 0.0 copy-start.1
  0.6 0.0 copy-start.2
  0.7 0.0 copy-start.3
  0.7 0.0 copy-start.8
  0.7 0.0 copy-start.9
  0.7 5.8 %forward_planes.1 = f32[1024,128]{1,0:T(8,128)S(1)} custom-call(bf16[32,256,256]{2,1,0:T(8,128)(2,1)} %bitcast.15, bf16[32,256,256]{2,1,0:T(8,128)(2,1)} %bitcast.16, bf16[128,256]{1,0:T(8,128)(2,1)} %constant.26.clone.tx_hbm, bf16[256,256]{1,0:T(8,128)(2,1)} %constant.27.clone.ty_hbm), custom_call_target="tpu_custom_call" | custom-call | flops 4000000000 | bytes 9000000 | tf_op jit(solution)/shard_map/forward_planes/pallas_call | solution.py:206
  6.5 30.0 %all_to_all.10 = f32[64,16,128]{2,1,0:T(8,128)S(1)} all-to-all(f32[64,16,128]{2,1,0:T(8,128)S(1)} %bitcast.12), channel_id=1, replica_groups=mesh['slab'=64,'group'=4] {'slab'}, dimensions={0} | all-to-all | bytes 1048576 | tf_op jit(solution)/shard_map/all_to_all | solution.py:434
  36.5 0.0 copy-start
  36.5 0.0 copy-done.1
  36.5 0.0 copy-done.2
  36.5 0.0 copy-done.3
  36.5 0.0 copy-done.8
  36.5 0.0 copy-done.9
  36.5 0.0 copy-start.6
  36.5 0.0 copy-start.7
  36.5 2.1 %middle_modes.1 = f32[512,128]{1,0:T(8,128)} custom-call(f32[1024,128]{1,0:T(8,128)S(1)} %bitcast.10, bf16[2,17,16,256]{3,2,1,0:T(8,128)(2,1)S(1)} %bitcast.14, bf16[48,384]{1,0:T(8,128)(2,1)S(1)} %copy-done.1, bf16[256,256]{1,0:T(8,128)(2,1)S(1)} %copy-done.8, bf16[512,512]{1,0:T(8,128)(2,1)S(1)} %copy-done.3, bf16[128,144]{1,0:T(8,128)(2,1)S(1)} %copy-done.9), custom_call_target="tpu_custom_call" | custom-call | flops 2000000000 | bytes 3000000 | tf_op jit(solution)/shard_map/middle_modes/pallas_call | solution.py:295
  38.6 6.1 %all-to-all-start.1 = ((f32[64,8,128]{2,1,0:T(8,128)}), f32[64,8,128]{2,1,0:T(8,128)S(1)}, u32[]{:S(2)}, u32[]{:S(2)}) async-start(f32[64,8,128]{2,1,0:T(8,128)} %bitcast.5), calls=%async_computation.1 | async-start | bytes 524288 | tf_op jit(solution)/shard_map/all_to_all | solution.py:434
  44.7 0.0 copy-done
  44.7 0.0 copy-start.4
  44.7 0.0 copy-start.5
  44.7 0.6 %input_modes.1 = (f32[24,256]{1,0:T(8,128)S(1)}, f32[24,256]{1,0:T(8,128)S(1)}, f32[24,256]{1,0:T(8,128)S(1)}, f32[24,256]{1,0:T(8,128)S(1)}) custom-call(s32[1]{0:T(128)} %bitcast.7.index_ref, f32[1024,128]{1,0:T(8,128)S(1)} %bitcast.11, bf16[48,384]{1,0:T(8,128)(2,1)S(1)} %copy-done.1, bf16[512,512]{1,0:T(8,128)(2,1)S(1)} %copy-done), custom_call_target="tpu_custom_call" | custom-call | flops 100000000 | bytes 1000000 | tf_op jit(solution)/shard_map/input_modes/pallas_call | solution.py:329
  45.3 0.1 collective-permute-start
  45.4 0.7 %collective-permute-start.1 = (f32[24,256]{1,0:T(8,128)S(1)}, f32[24,256]{1,0:T(8,128)S(1)}, u32[]{:S(2)}, u32[]{:S(2)}) collective-permute-start(f32[24,256]{1,0:T(8,128)S(1)} %get-tuple-element.10), channel_id=1, source_target_pairs={{0,2},{1,3},{2,0},{3,1},{4,6},{5,7},{6,4},{7,5},{8,10},{9,11},{10,... | collective-permute-start | bytes 73736 | tf_op jit(solution)/shard_map/ppermute | solution.py:444
  46.2 2.6 %collective-permute-start.2 = (f32[24,256]{1,0:T(8,128)S(1)}, f32[24,256]{1,0:T(8,128)S(1)}, u32[]{:S(2)}, u32[]{:S(2)}) collective-permute-start(f32[24,256]{1,0:T(8,128)S(1)} %get-tuple-element.11), channel_id=1, source_target_pairs={{0,3},{1,2},{2,1},{3,0},{4,7},{5,6},{6,5},{7,4},{8,11},{9,10},{10,... | collective-permute-start | bytes 73736 | tf_op jit(solution)/shard_map/ppermute | solution.py:444
  48.8 0.0 collective-permute-done.b_ref
  48.8 2.7 %collective-permute-done.1.c_ref = f32[24,256]{1,0:T(8,128)S(1)} collective-permute-done((f32[24,256]{1,0:T(8,128)S(1)}, f32[24,256]{1,0:T(8,128)S(1)}, u32[]{:S(2)}, u32[]{:S(2)}) %collective-permute-start.1) | collective-permute-done | bytes 24608 | tf_op jit(solution)/shard_map/ppermute | solution.py:444
  51.5 0.1 collective-permute-done.2.d_ref
  51.7 0.0 copy-done.6
  51.7 0.0 copy-done.7
  51.7 0.6 weight_terms.1.terms_ref
  52.2 5.0 %all-to-all-done.1 = f32[64,8,128]{2,1,0:T(8,128)S(1)} async-done(((f32[64,8,128]{2,1,0:T(8,128)}), f32[64,8,128]{2,1,0:T(8,128)S(1)}, u32[]{:S(2)}, u32[]{:S(2)}) %all-to-all-start.1) | async-done | bytes 262176 | tf_op jit(solution)/shard_map/all_to_all | solution.py:434
  57.2 0.0 copy-done.4
  57.2 0.0 copy-done.5
  57.3 2.8 %back_planes.1 = (bf16[8,4,256,256]{3,2,1,0:T(8,128)(2,1)}, f32[2,17,4,256]{3,2,1,0:T(4,128)}) custom-call(f32[512,128]{1,0:T(8,128)S(1)} %bitcast.13, bf16[256,512]{1,0:T(8,128)(2,1)S(1)} %copy-done.4, bf16[256,192]{1,0:T(8,128)(2,1)S(1)} %copy-done.5, f32[2,17,4,256]{3,2,1,0:T(4,128)S(1)} %weight_terms.1.terms_ref), custom_call_target="tpu_custom_call" | custom-call | flops 4000000000 | bytes 6000000 | tf_op jit(solution)/shard_map/back_planes/pallas_call | solution.py:413
Async XLA Ops:
  0.6 35.8 %copy-start.1 = (bf16[48,384]{1,0:T(8,128)(2,1)S(1)}, bf16[48,384]{1,0:T(8,128)(2,1)}, u32[]{:S(2)}) copy-start(bf16[48,384]{1,0:T(8,128)(2,1)} %constant.28.clone.tz_ref) | copy-start | bytes 110596
  0.6 35.8 %copy-start.2 = (bf16[2,16,17,256]{3,1,2,0:T(8,128)(2,1)S(1)}, bf16[2,16,17,256]{3,1,2,0:T(8,128)(2,1)}, u32[]{:S(2)}) copy-start(bf16[2,16,17,256]{3,1,2,0:T(8,128)(2,1)} %param.17) | copy-start | bytes 835588
  0.7 35.8 %copy-start.3 = (bf16[512,512]{1,0:T(8,128)(2,1)S(1)}, bf16[512,512]{1,0:T(8,128)(2,1)}, u32[]{:S(2)}) copy-start(bf16[512,512]{1,0:T(8,128)(2,1)} %constant.30.clone.c_ref) | copy-start | bytes 1572868
  0.7 35.8 %copy-start.8 = (bf16[256,256]{1,0:T(8,128)(2,1)S(1)}, bf16[256,256]{1,0:T(8,128)(2,1)}, u32[]{:S(2)}) copy-start(bf16[256,256]{1,0:T(8,128)(2,1)} %constant.29.clone.e_ref) | copy-start | bytes 393220
  0.7 35.8 %copy-start.9 = (bf16[128,144]{1,0:T(8,128)(2,1)S(1)}, bf16[128,144]{1,0:T(8,128)(2,1)}, u32[]{:S(2)}) copy-start(bf16[128,144]{1,0:T(8,128)(2,1)} %constant.31.clone.tb_ref) | copy-start | bytes 110596
  36.5 8.2 %copy-start = (bf16[512,512]{1,0:T(8,128)(2,1)S(1)}, bf16[512,512]{1,0:T(8,128)(2,1)}, u32[]{:S(2)}) copy-start(bf16[512,512]{1,0:T(8,128)(2,1)} %constant.32.clone.cut_ref) | copy-start | bytes 1572868
  36.5 15.2 %copy-start.6 = (bf16[128,512]{1,0:T(8,128)(2,1)S(1)}, bf16[128,512]{1,0:T(8,128)(2,1)}, u32[]{:S(2)}) copy-start(bf16[128,512]{1,0:T(8,128)(2,1)} %constant.34.clone.eg_ref) | copy-start | bytes 393220
  36.5 15.2 %copy-start.7 = (bf16[128,512]{1,0:T(8,128)(2,1)S(1)}, bf16[128,512]{1,0:T(8,128)(2,1)}, u32[]{:S(2)}) copy-start(bf16[128,512]{1,0:T(8,128)(2,1)} %constant.33.clone.eu_ref) | copy-start | bytes 393220
  38.6 18.6 %all-to-all-start.1 = ((f32[64,8,128]{2,1,0:T(8,128)}), f32[64,8,128]{2,1,0:T(8,128)S(1)}, u32[]{:S(2)}, u32[]{:S(2)}) async-start(f32[64,8,128]{2,1,0:T(8,128)} %bitcast.5), calls=%async_computation.1 | async-start | bytes 524288 | tf_op jit(solution)/shard_map/all_to_all | solution.py:434
  44.7 12.6 %copy-start.4 = (bf16[256,512]{1,0:T(8,128)(2,1)S(1)}, bf16[256,512]{1,0:T(8,128)(2,1)}, u32[]{:S(2)}) copy-start(bf16[256,512]{1,0:T(8,128)(2,1)} %constant.35.clone.ty_ref) | copy-start | bytes 786436
  44.7 12.5 %copy-start.5 = (bf16[256,192]{1,0:T(8,128)(2,1)S(1)}, bf16[256,192]{1,0:T(8,128)(2,1)}, u32[]{:S(2)}) copy-start(bf16[256,192]{1,0:T(8,128)(2,1)} %constant.36.clone.tx_ref) | copy-start | bytes 294916
  45.3 3.5 %collective-permute-start = (f32[24,256]{1,0:T(8,128)S(1)}, f32[24,256]{1,0:T(8,128)S(1)}, u32[]{:S(2)}, u32[]{:S(2)}) collective-permute-start(f32[24,256]{1,0:T(8,128)S(1)} %get-tuple-element.9), channel_id=1, source_target_pairs={{0,1},{1,0},{2,3},{3,2},{4,5},{5,4},{6,7},{7,6},{8,9},{9,8},{10,11... | collective-permute-start | bytes 73736 | tf_op jit(solution)/shard_map/ppermute | solution.py:444
  45.4 6.1 %collective-permute-start.1 = (f32[24,256]{1,0:T(8,128)S(1)}, f32[24,256]{1,0:T(8,128)S(1)}, u32[]{:S(2)}, u32[]{:S(2)}) collective-permute-start(f32[24,256]{1,0:T(8,128)S(1)} %get-tuple-element.10), channel_id=1, source_target_pairs={{0,2},{1,3},{2,0},{3,1},{4,6},{5,7},{6,4},{7,5},{8,10},{9,11},{10,... | collective-permute-start | bytes 73736 | tf_op jit(solution)/shard_map/ppermute | solution.py:444
  46.2 5.5 %collective-permute-start.2 = (f32[24,256]{1,0:T(8,128)S(1)}, f32[24,256]{1,0:T(8,128)S(1)}, u32[]{:S(2)}, u32[]{:S(2)}) collective-permute-start(f32[24,256]{1,0:T(8,128)S(1)} %get-tuple-element.11), channel_id=1, source_target_pairs={{0,3},{1,2},{2,1},{3,0},{4,7},{5,6},{6,5},{7,4},{8,11},{9,10},{10,... | collective-permute-start | bytes 73736 | tf_op jit(solution)/shard_map/ppermute | solution.py:444

commit v4 on v3

--- a/solution.py
+++ b/solution.py
@@ -156,7 +156,7 @@
 
 
 STEPS = 16
-WAITS = (1, 1, 2, 4, 8)
+WAITS = (2, 3, 4, 7)
 
 
 def forward_kernel(cot_hbm, fld_hbm, tx_hbm, ty_hbm, out_ref, field_ref, tx_ref, ty_ref, rows_ref, sems):
@@ -179,26 +179,31 @@
         parts = [dot(field_ref[i * 4 + c4], ty_ref[...]) for c4 in range(4)]
         rows = jnp.where(slot == 0, parts[0], jnp.where(slot == 1, parts[1], jnp.where(slot == 2, parts[2], parts[3])))
         high, low = split(rows)
-        rows_ref[i % 2, 0] = high
-        rows_ref[i % 2, 1] = low
-
-    def spectrum(i):
-        mixed = dot(tx_ref[...], rows_ref[i % 2, 0])
-        mixed = mixed[:64] + mixed[64:] + dot(tx_ref[:64], rows_ref[i % 2, 1])
-        result = mixed[:KX] + sign * swap_parts(mixed[KX:])
-        for half in range(2):
-            out_ref[pl.ds(half * 16 + i, KX, stride=32), :] = result[:, half * 128:(half + 1) * 128]
-
-    first = 0
+        rows_ref[0, :, i * 256:(i + 1) * 256] = high
+        rows_ref[1, :, i * 256:(i + 1) * 256] = low
+
+    def spectra(start, count):
+        lanes = slice(start * 256, (start + count) * 256)
+        mixed = dot(tx_ref[...], rows_ref[0, :, lanes])
+        mixed = mixed[:64] + mixed[64:] + dot(tx_ref[:64], rows_ref[1, :, lanes])
+        for j in range(count):
+            both = mixed[:, j * 256:(j + 1) * 256]
+            result = both[:KX] + sign * swap_parts(both[KX:])
+            for half in range(2):
+                row = half * 16 + start + j
+                out_ref[pl.ds(row, KX, stride=32), :] = result[:, half * 128:(half + 1) * 128]
+
+    first, ready = 0, (0, 0)
     for count in WAITS:
         for i in range(first, first + count):
             blocks[i].wait()
         for i in range(first, first + count):
             rows_y(i)
-            if i > 0:
-                spectrum(i - 1)
+        if ready[1]:
+            spectra(*ready)
+        ready = (first, count)
         first += count
-    spectrum(STEPS - 1)
+    spectra(*ready)
 
 
 def forward(cotangent, field_in):
@@ -211,7 +216,7 @@
             pltpu.VMEM((STEPS * 4, NX, NY), bf16),
             pltpu.VMEM((128, NX), bf16),
             pltpu.VMEM((NY, 256), bf16),
-            pltpu.VMEM((2, 2, NX, 256), bf16),
+            pltpu.VMEM((2, NX, STEPS * 256), bf16),
             pltpu.SemaphoreType.DMA((STEPS + 2,)),
         ],
         compiler_params=pltpu.CompilerParams(vmem_limit_bytes=60 * 1024 * 1024),

time: 60.3 us -> 60 us (level)
  no operation moved by 1% of the time
where the time goes in v4:
time: 60 us; the launch traced here: 59.8 us
  blocking collectives  30 us (50%)
  Pallas kernels  11.6 us (19%)
  starting transfers between devices  9.52 us (16%)
  waiting for transfers between devices  7.86 us (13%)
  between operations  0.78 us (1%)
    all_to_all x1, blocking collectives, exchange(): lax.all_to_all(chunks.reshape(SLABS, rows, 128), 'slab', 0, 0, tiled=True)  30 us
    all_to_all x1, starting transfers between devices, exchange(): lax.all_to_all(chunks.reshape(SLABS, rows, 128), 'slab', 0, 0, tiled=True)  6.06 us
    pallas_call x1, Pallas kernels, forward(): pl.pallas_call(forward_kernel, out_shape=pltpu.VMEM((SLABS * 16, 128), f3...  5.46 us
    all_to_all x1, waiting for transfers between devices, exchange(): lax.all_to_all(chunks.reshape(SLABS, rows, 128), 'slab', 0, 0, tiled=True)  5.02 us
    ppermute x3, starting transfers between devices, body(): pieces[k] = lax.ppermute(pieces[k], 'group', [(i, i ^ k) for i in range(4)])  3.46 us
    pallas_call x1, Pallas kernels, back(): pl.pallas_call(back_kernel, out_shape=(jax.ShapeDtypeStruct((8, 4, NX, NY...  2.84 us
    ppermute x3, waiting for transfers between devices, body(): pieces[k] = lax.ppermute(pieces[k], 'group', [(i, i ^ k) for i in range(4)])  2.84 us
    pallas_call x1, Pallas kernels, middle(): pl.pallas_call(middle_kernel, out_shape=pltpu.VMEM((SLABS * 8, 128), f32)...  2.1 us
  transfers between devices with their start and end apart: 4, of which 3 were waited for; matrix products, arithmetic and copies ran while one was open for 0% of the time, Pallas kernels for 2%

profile of v4, /device:TPU:16, one launch (start us, length us, event | category | flops | bytes accessed | tf_op | source)
XLA Modules:
  0.0 59.8 jit_solution(14467629281199315046)
XLA Ops:
  0.6 0.0 copy-start.1
  0.6 0.0 copy-start.2
  0.7 0.0 copy-start.3
  0.7 0.0 copy-start.8
  0.7 0.0 copy-start.9
  0.7 5.5 %forward_planes.1 = f32[1024,128]{1,0:T(8,128)S(1)} custom-call(bf16[32,256,256]{2,1,0:T(8,128)(2,1)} %bitcast.15, bf16[32,256,256]{2,1,0:T(8,128)(2,1)} %bitcast.16, bf16[128,256]{1,0:T(8,128)(2,1)} %constant.26.clone.tx_hbm, bf16[256,256]{1,0:T(8,128)(2,1)} %constant.27.clone.ty_hbm), custom_call_target="tpu_custom_call" | custom-call | flops 4000000000 | bytes 9000000 | tf_op jit(solution)/shard_map/forward_planes/pallas_call | solution.py:211
  6.2 30.0 %all_to_all.10 = f32[64,16,128]{2,1,0:T(8,128)S(1)} all-to-all(f32[64,16,128]{2,1,0:T(8,128)S(1)} %bitcast.12), channel_id=1, replica_groups=mesh['slab'=64,'group'=4] {'slab'}, dimensions={0} | all-to-all | bytes 1048576 | tf_op jit(solution)/shard_map/all_to_all | solution.py:439
  36.2 0.0 copy-start
  36.2 0.0 copy-done.1
  36.2 0.0 copy-done.2
  36.2 0.0 copy-done.3
  36.2 0.0 copy-done.8
  36.2 0.0 copy-done.9
  36.2 0.0 copy-start.6
  36.2 0.0 copy-start.7
  36.2 2.1 %middle_modes.1 = f32[512,128]{1,0:T(8,128)} custom-call(f32[1024,128]{1,0:T(8,128)S(1)} %bitcast.10, bf16[2,17,16,256]{3,2,1,0:T(8,128)(2,1)S(1)} %bitcast.14, bf16[48,384]{1,0:T(8,128)(2,1)S(1)} %copy-done.1, bf16[256,256]{1,0:T(8,128)(2,1)S(1)} %copy-done.8, bf16[512,512]{1,0:T(8,128)(2,1)S(1)} %copy-done.3, bf16[128,144]{1,0:T(8,128)(2,1)S(1)} %copy-done.9), custom_call_target="tpu_custom_call" | custom-call | flops 2000000000 | bytes 3000000 | tf_op jit(solution)/shard_map/middle_modes/pallas_call | solution.py:300
  38.3 6.1 %all-to-all-start.1 = ((f32[64,8,128]{2,1,0:T(8,128)}), f32[64,8,128]{2,1,0:T(8,128)S(1)}, u32[]{:S(2)}, u32[]{:S(2)}) async-start(f32[64,8,128]{2,1,0:T(8,128)} %bitcast.5), calls=%async_computation.1 | async-start | bytes 524288 | tf_op jit(solution)/shard_map/all_to_all | solution.py:439
  44.4 0.0 copy-done
  44.4 0.0 copy-start.4
  44.4 0.0 copy-start.5
  44.4 0.6 %input_modes.1 = (f32[24,256]{1,0:T(8,128)S(1)}, f32[24,256]{1,0:T(8,128)S(1)}, f32[24,256]{1,0:T(8,128)S(1)}, f32[24,256]{1,0:T(8,128)S(1)}) custom-call(s32[1]{0:T(128)} %bitcast.7.index_ref, f32[1024,128]{1,0:T(8,128)S(1)} %bitcast.11, bf16[48,384]{1,0:T(8,128)(2,1)S(1)} %copy-done.1, bf16[512,512]{1,0:T(8,128)(2,1)S(1)} %copy-done), custom_call_target="tpu_custom_call" | custom-call | flops 100000000 | bytes 1000000 | tf_op jit(solution)/shard_map/input_modes/pallas_call | solution.py:334
  45.0 0.1 collective-permute-start
  45.1 0.7 %collective-permute-start.1 = (f32[24,256]{1,0:T(8,128)S(1)}, f32[24,256]{1,0:T(8,128)S(1)}, u32[]{:S(2)}, u32[]{:S(2)}) collective-permute-start(f32[24,256]{1,0:T(8,128)S(1)} %get-tuple-element.10), channel_id=1, source_target_pairs={{0,2},{1,3},{2,0},{3,1},{4,6},{5,7},{6,4},{7,5},{8,10},{9,11},{10,... | collective-permute-start | bytes 73736 | tf_op jit(solution)/shard_map/ppermute | solution.py:449
  45.9 2.7 %collective-permute-start.2 = (f32[24,256]{1,0:T(8,128)S(1)}, f32[24,256]{1,0:T(8,128)S(1)}, u32[]{:S(2)}, u32[]{:S(2)}) collective-permute-start(f32[24,256]{1,0:T(8,128)S(1)} %get-tuple-element.11), channel_id=1, source_target_pairs={{0,3},{1,2},{2,1},{3,0},{4,7},{5,6},{6,5},{7,4},{8,11},{9,10},{10,... | collective-permute-start | bytes 73736 | tf_op jit(solution)/shard_map/ppermute | solution.py:449
  48.5 0.0 collective-permute-done.b_ref
  48.5 2.7 %collective-permute-done.1.c_ref = f32[24,256]{1,0:T(8,128)S(1)} collective-permute-done((f32[24,256]{1,0:T(8,128)S(1)}, f32[24,256]{1,0:T(8,128)S(1)}, u32[]{:S(2)}, u32[]{:S(2)}) %collective-permute-start.1) | collective-permute-done | bytes 24608 | tf_op jit(solution)/shard_map/ppermute | solution.py:449
  51.2 0.1 collective-permute-done.2.d_ref
  51.3 0.0 copy-done.6
  51.3 0.0 copy-done.7
  51.4 0.6 weight_terms.1.terms_ref
  51.9 5.0 %all-to-all-done.1 = f32[64,8,128]{2,1,0:T(8,128)S(1)} async-done(((f32[64,8,128]{2,1,0:T(8,128)}), f32[64,8,128]{2,1,0:T(8,128)S(1)}, u32[]{:S(2)}, u32[]{:S(2)}) %all-to-all-start.1) | async-done | bytes 262176 | tf_op jit(solution)/shard_map/all_to_all | solution.py:439
  56.9 0.0 copy-done.4
  56.9 0.0 copy-done.5
  56.9 2.8 %back_planes.1 = (bf16[8,4,256,256]{3,2,1,0:T(8,128)(2,1)}, f32[2,17,4,256]{3,2,1,0:T(4,128)}) custom-call(f32[512,128]{1,0:T(8,128)S(1)} %bitcast.13, bf16[256,512]{1,0:T(8,128)(2,1)S(1)} %copy-done.4, bf16[256,192]{1,0:T(8,128)(2,1)S(1)} %copy-done.5, f32[2,17,4,256]{3,2,1,0:T(4,128)S(1)} %weight_terms.1.terms_ref), custom_call_target="tpu_custom_call" | custom-call | flops 4000000000 | bytes 6000000 | tf_op jit(solution)/shard_map/back_planes/pallas_call | solution.py:418
Async XLA Ops:
  0.6 35.5 %copy-start.1 = (bf16[48,384]{1,0:T(8,128)(2,1)S(1)}, bf16[48,384]{1,0:T(8,128)(2,1)}, u32[]{:S(2)}) copy-start(bf16[48,384]{1,0:T(8,128)(2,1)} %constant.28.clone.tz_ref) | copy-start | bytes 110596
  0.6 35.5 %copy-start.2 = (bf16[2,16,17,256]{3,1,2,0:T(8,128)(2,1)S(1)}, bf16[2,16,17,256]{3,1,2,0:T(8,128)(2,1)}, u32[]{:S(2)}) copy-start(bf16[2,16,17,256]{3,1,2,0:T(8,128)(2,1)} %param.17) | copy-start | bytes 835588
  0.7 35.5 %copy-start.3 = (bf16[512,512]{1,0:T(8,128)(2,1)S(1)}, bf16[512,512]{1,0:T(8,128)(2,1)}, u32[]{:S(2)}) copy-start(bf16[512,512]{1,0:T(8,128)(2,1)} %constant.30.clone.c_ref) | copy-start | bytes 1572868
  0.7 35.5 %copy-start.8 = (bf16[256,256]{1,0:T(8,128)(2,1)S(1)}, bf16[256,256]{1,0:T(8,128)(2,1)}, u32[]{:S(2)}) copy-start(bf16[256,256]{1,0:T(8,128)(2,1)} %constant.29.clone.e_ref) | copy-start | bytes 393220
  0.7 35.5 %copy-start.9 = (bf16[128,144]{1,0:T(8,128)(2,1)S(1)}, bf16[128,144]{1,0:T(8,128)(2,1)}, u32[]{:S(2)}) copy-start(bf16[128,144]{1,0:T(8,128)(2,1)} %constant.31.clone.tb_ref) | copy-start | bytes 110596
  36.2 8.2 %copy-start = (bf16[512,512]{1,0:T(8,128)(2,1)S(1)}, bf16[512,512]{1,0:T(8,128)(2,1)}, u32[]{:S(2)}) copy-start(bf16[512,512]{1,0:T(8,128)(2,1)} %constant.32.clone.cut_ref) | copy-start | bytes 1572868
  36.2 15.2 %copy-start.6 = (bf16[128,512]{1,0:T(8,128)(2,1)S(1)}, bf16[128,512]{1,0:T(8,128)(2,1)}, u32[]{:S(2)}) copy-start(bf16[128,512]{1,0:T(8,128)(2,1)} %constant.34.clone.eg_ref) | copy-start | bytes 393220
  36.2 15.1 %copy-start.7 = (bf16[128,512]{1,0:T(8,128)(2,1)S(1)}, bf16[128,512]{1,0:T(8,128)(2,1)}, u32[]{:S(2)}) copy-start(bf16[128,512]{1,0:T(8,128)(2,1)} %constant.33.clone.eu_ref) | copy-start | bytes 393220
  38.3 18.6 %all-to-all-start.1 = ((f32[64,8,128]{2,1,0:T(8,128)}), f32[64,8,128]{2,1,0:T(8,128)S(1)}, u32[]{:S(2)}, u32[]{:S(2)}) async-start(f32[64,8,128]{2,1,0:T(8,128)} %bitcast.5), calls=%async_computation.1 | async-start | bytes 524288 | tf_op jit(solution)/shard_map/all_to_all | solution.py:439
  44.4 12.6 %copy-start.4 = (bf16[256,512]{1,0:T(8,128)(2,1)S(1)}, bf16[256,512]{1,0:T(8,128)(2,1)}, u32[]{:S(2)}) copy-start(bf16[256,512]{1,0:T(8,128)(2,1)} %constant.35.clone.ty_ref) | copy-start | bytes 786436
  44.4 12.5 %copy-start.5 = (bf16[256,192]{1,0:T(8,128)(2,1)S(1)}, bf16[256,192]{1,0:T(8,128)(2,1)}, u32[]{:S(2)}) copy-start(bf16[256,192]{1,0:T(8,128)(2,1)} %constant.36.clone.tx_ref) | copy-start | bytes 294916
  45.0 3.5 %collective-permute-start = (f32[24,256]{1,0:T(8,128)S(1)}, f32[24,256]{1,0:T(8,128)S(1)}, u32[]{:S(2)}, u32[]{:S(2)}) collective-permute-start(f32[24,256]{1,0:T(8,128)S(1)} %get-tuple-element.9), channel_id=1, source_target_pairs={{0,1},{1,0},{2,3},{3,2},{4,5},{5,4},{6,7},{7,6},{8,9},{9,8},{10,11... | collective-permute-start | bytes 73736 | tf_op jit(solution)/shard_map/ppermute | solution.py:449
  45.1 6.1 %collective-permute-start.1 = (f32[24,256]{1,0:T(8,128)S(1)}, f32[24,256]{1,0:T(8,128)S(1)}, u32[]{:S(2)}, u32[]{:S(2)}) collective-permute-start(f32[24,256]{1,0:T(8,128)S(1)} %get-tuple-element.10), channel_id=1, source_target_pairs={{0,2},{1,3},{2,0},{3,1},{4,6},{5,7},{6,4},{7,5},{8,10},{9,11},{10,... | collective-permute-start | bytes 73736 | tf_op jit(solution)/shard_map/ppermute | solution.py:449
  45.9 5.5 %collective-permute-start.2 = (f32[24,256]{1,0:T(8,128)S(1)}, f32[24,256]{1,0:T(8,128)S(1)}, u32[]{:S(2)}, u32[]{:S(2)}) collective-permute-start(f32[24,256]{1,0:T(8,128)S(1)} %get-tuple-element.11), channel_id=1, source_target_pairs={{0,3},{1,2},{2,1},{3,0},{4,7},{5,6},{6,5},{7,4},{8,11},{9,10},{10,... | collective-permute-start | bytes 73736 | tf_op jit(solution)/shard_map/ppermute | solution.py:449

commit v5 on v4

--- a/solution.py
+++ b/solution.py
@@ -96,10 +96,10 @@
 
 
 def collect_table():
-    row, col = np.arange(512), np.arange(512)
-    channel = col // 128 * 4 + col // 32 % 4
-    hit = (row // 256)[:, None] == (col // 16 % 2)[None]
-    return (hit & ((row // 16 % 16)[:, None] == channel[None])).astype(ml_dtypes.bfloat16)
+    row, col = np.arange(256), np.arange(256)
+    hit = (row // 128)[:, None] == (col // 128)[None]
+    hit = hit & ((row // 64 % 2)[:, None] == (col // 16 % 2)[None])
+    return (hit & ((row // 16 % 4)[:, None] == (col // 32 % 4)[None])).astype(ml_dtypes.bfloat16)
 
 
 def quarter_table():
@@ -274,8 +274,17 @@
         g_r = wide[kz * HALF:(kz + 1) * HALF]
         g_i = wide[(KZ + kz) * HALF:(KZ + kz + 1) * HALF]
         w_r, w_i = w_ref[0, kz].astype(f32), w_ref[1, kz].astype(f32)
-        products.append(jnp.concatenate([g_r * w_r + g_i * w_i, g_i * w_r - g_r * w_i], 1))
-    sums = precise_dot(jnp.concatenate(products, 0), c_ref[...])
+        products.append((g_r * w_r + g_i * w_i, g_i * w_r - g_r * w_i))
+    left_half = lane_iota(HALF, 128) < 64
+    halves = []
+    for pair in range(2):
+        cut = slice(pair * 128, (pair + 1) * 128)
+        for real, imag in products:
+            first = jnp.where(left_half, real[:, cut], roll_half(imag[:, cut]))
+            second = jnp.where(left_half, roll_half(real[:, cut]), imag[:, cut])
+            halves.append(jnp.concatenate([first, second], 1))
+    sums = precise_dot(jnp.concatenate(halves, 0), c_ref[...])
+    sums = jnp.concatenate([sums[:KZ * HALF], sums[KZ * HALF:]], 1)
     own = jnp.concatenate([own, own], 1)
     sum_ref[...] = jnp.zeros_like(sum_ref)
     for kz in range(KZ):

time: 60 us -> 60 us (level)
  no operation moved by 1% of the time
where the time goes in v5:
time: 60 us; the launch traced here: 59.8 us
  blocking collectives  30 us (50%)
  Pallas kernels  11.6 us (19%)
  starting transfers between devices  9.53 us (16%)
  waiting for transfers between devices  7.85 us (13%)
  between operations  0.78 us (1%)
    all_to_all x1, blocking collectives, exchange(): lax.all_to_all(chunks.reshape(SLABS, rows, 128), 'slab', 0, 0, tiled=True)  30 us
    all_to_all x1, starting transfers between devices, exchange(): lax.all_to_all(chunks.reshape(SLABS, rows, 128), 'slab', 0, 0, tiled=True)  6.06 us
    pallas_call x1, Pallas kernels, forward(): pl.pallas_call(forward_kernel, out_shape=pltpu.VMEM((SLABS * 16, 128), f3...  5.43 us
    all_to_all x1, waiting for transfers between devices, exchange(): lax.all_to_all(chunks.reshape(SLABS, rows, 128), 'slab', 0, 0, tiled=True)  5.02 us
    ppermute x3, starting transfers between devices, body(): pieces[k] = lax.ppermute(pieces[k], 'group', [(i, i ^ k) for i in range(4)])  3.46 us
    pallas_call x1, Pallas kernels, back(): pl.pallas_call(back_kernel, out_shape=(jax.ShapeDtypeStruct((8, 4, NX, NY...  2.84 us
    ppermute x3, waiting for transfers between devices, body(): pieces[k] = lax.ppermute(pieces[k], 'group', [(i, i ^ k) for i in range(4)])  2.84 us
    pallas_call x1, Pallas kernels, middle(): pl.pallas_call(middle_kernel, out_shape=pltpu.VMEM((SLABS * 8, 128), f32)...  2.12 us
  transfers between devices with their start and end apart: 4, of which 3 were waited for; matrix products, arithmetic and copies ran while one was open for 0% of the time, Pallas kernels for 2%

profile of v5, /device:TPU:16, one launch (start us, length us, event | category | flops | bytes accessed | tf_op | source)
XLA Modules:
  0.0 59.8 jit_solution(3646864806034215024)
XLA Ops:
  0.6 0.0 copy-start.1
  0.6 0.0 copy-start.2
  0.7 0.0 copy-start.7
  0.7 0.0 copy-start.8
  0.7 0.0 copy-start.9
  0.7 5.4 %forward_planes.1 = f32[1024,128]{1,0:T(8,128)S(1)} custom-call(bf16[32,256,256]{2,1,0:T(8,128)(2,1)} %bitcast.15, bf16[32,256,256]{2,1,0:T(8,128)(2,1)} %bitcast.16, bf16[128,256]{1,0:T(8,128)(2,1)} %constant.26.clone.tx_hbm, bf16[256,256]{1,0:T(8,128)(2,1)} %constant.27.clone.ty_hbm), custom_call_target="tpu_custom_call" | custom-call | flops 4000000000 | bytes 9000000 | tf_op jit(solution)/shard_map/forward_planes/pallas_call | solution.py:211
  6.1 30.0 %all_to_all.10 = f32[64,16,128]{2,1,0:T(8,128)S(1)} all-to-all(f32[64,16,128]{2,1,0:T(8,128)S(1)} %bitcast.12), channel_id=1, replica_groups=mesh['slab'=64,'group'=4] {'slab'}, dimensions={0} | all-to-all | bytes 1048576 | tf_op jit(solution)/shard_map/all_to_all | solution.py:448
  36.1 0.0 copy-start
  36.1 0.0 copy-done.1
  36.1 0.0 copy-done.2
  36.1 0.0 copy-done.7
  36.1 0.0 copy-done.8
  36.2 0.0 copy-done.9
  36.2 0.0 copy-start.5
  36.2 0.0 copy-start.6
  36.2 2.1 %middle_modes.1 = f32[512,128]{1,0:T(8,128)} custom-call(f32[1024,128]{1,0:T(8,128)S(1)} %bitcast.10, bf16[2,17,16,256]{3,2,1,0:T(8,128)(2,1)S(1)} %bitcast.14, bf16[48,384]{1,0:T(8,128)(2,1)S(1)} %copy-done.1, bf16[256,256]{1,0:T(8,128)(2,1)S(1)} %copy-done.8, bf16[256,256]{1,0:T(8,128)(2,1)S(1)} %copy-done.7, bf16[128,144]{1,0:T(8,128)(2,1)S(1)} %copy-done.9), custom_call_target="tpu_custom_call" | custom-call | flops 2000000000 | bytes 3000000 | tf_op jit(solution)/shard_map/middle_modes/pallas_call | solution.py:309
  38.3 6.1 %all-to-all-start.1 = ((f32[64,8,128]{2,1,0:T(8,128)}), f32[64,8,128]{2,1,0:T(8,128)S(1)}, u32[]{:S(2)}, u32[]{:S(2)}) async-start(f32[64,8,128]{2,1,0:T(8,128)} %bitcast.5), calls=%async_computation.1 | async-start | bytes 524288 | tf_op jit(solution)/shard_map/all_to_all | solution.py:448
  44.4 0.0 copy-done
  44.4 0.0 copy-start.3
  44.4 0.0 copy-start.4
  44.4 0.6 %input_modes.1 = (f32[24,256]{1,0:T(8,128)S(1)}, f32[24,256]{1,0:T(8,128)S(1)}, f32[24,256]{1,0:T(8,128)S(1)}, f32[24,256]{1,0:T(8,128)S(1)}) custom-call(s32[1]{0:T(128)} %bitcast.7.index_ref, f32[1024,128]{1,0:T(8,128)S(1)} %bitcast.11, bf16[48,384]{1,0:T(8,128)(2,1)S(1)} %copy-done.1, bf16[512,512]{1,0:T(8,128)(2,1)S(1)} %copy-done), custom_call_target="tpu_custom_call" | custom-call | flops 100000000 | bytes 1000000 | tf_op jit(solution)/shard_map/input_modes/pallas_call | solution.py:343
  45.0 0.1 collective-permute-start
  45.1 0.7 %collective-permute-start.1 = (f32[24,256]{1,0:T(8,128)S(1)}, f32[24,256]{1,0:T(8,128)S(1)}, u32[]{:S(2)}, u32[]{:S(2)}) collective-permute-start(f32[24,256]{1,0:T(8,128)S(1)} %get-tuple-element.10), channel_id=1, source_target_pairs={{0,2},{1,3},{2,0},{3,1},{4,6},{5,7},{6,4},{7,5},{8,10},{9,11},{10,... | collective-permute-start | bytes 73736 | tf_op jit(solution)/shard_map/ppermute | solution.py:458
  45.9 2.7 %collective-permute-start.2 = (f32[24,256]{1,0:T(8,128)S(1)}, f32[24,256]{1,0:T(8,128)S(1)}, u32[]{:S(2)}, u32[]{:S(2)}) collective-permute-start(f32[24,256]{1,0:T(8,128)S(1)} %get-tuple-element.11), channel_id=1, source_target_pairs={{0,3},{1,2},{2,1},{3,0},{4,7},{5,6},{6,5},{7,4},{8,11},{9,10},{10,... | collective-permute-start | bytes 73736 | tf_op jit(solution)/shard_map/ppermute | solution.py:458
  48.5 0.0 collective-permute-done.b_ref
  48.5 2.7 %collective-permute-done.1.c_ref = f32[24,256]{1,0:T(8,128)S(1)} collective-permute-done((f32[24,256]{1,0:T(8,128)S(1)}, f32[24,256]{1,0:T(8,128)S(1)}, u32[]{:S(2)}, u32[]{:S(2)}) %collective-permute-start.1) | collective-permute-done | bytes 24608 | tf_op jit(solution)/shard_map/ppermute | solution.py:458
  51.2 0.1 collective-permute-done.2.d_ref
  51.4 0.0 copy-done.5
  51.4 0.0 copy-done.6
  51.4 0.6 weight_terms.1.terms_ref
  51.9 5.0 %all-to-all-done.1 = f32[64,8,128]{2,1,0:T(8,128)S(1)} async-done(((f32[64,8,128]{2,1,0:T(8,128)}), f32[64,8,128]{2,1,0:T(8,128)S(1)}, u32[]{:S(2)}, u32[]{:S(2)}) %all-to-all-start.1) | async-done | bytes 262176 | tf_op jit(solution)/shard_map/all_to_all | solution.py:448
  56.9 0.0 copy-done.3
  56.9 0.0 copy-done.4
  56.9 2.8 %back_planes.1 = (bf16[8,4,256,256]{3,2,1,0:T(8,128)(2,1)}, f32[2,17,4,256]{3,2,1,0:T(4,128)}) custom-call(f32[512,128]{1,0:T(8,128)S(1)} %bitcast.13, bf16[256,512]{1,0:T(8,128)(2,1)S(1)} %copy-done.3, bf16[256,192]{1,0:T(8,128)(2,1)S(1)} %copy-done.4, f32[2,17,4,256]{3,2,1,0:T(4,128)S(1)} %weight_terms.1.terms_ref), custom_call_target="tpu_custom_call" | custom-call | flops 4000000000 | bytes 6000000 | tf_op jit(solution)/shard_map/back_planes/pallas_call | solution.py:427
Async XLA Ops:
  0.6 35.5 %copy-start.1 = (bf16[48,384]{1,0:T(8,128)(2,1)S(1)}, bf16[48,384]{1,0:T(8,128)(2,1)}, u32[]{:S(2)}) copy-start(bf16[48,384]{1,0:T(8,128)(2,1)} %constant.28.clone.tz_ref) | copy-start | bytes 110596
  0.6 35.5 %copy-start.2 = (bf16[2,16,17,256]{3,1,2,0:T(8,128)(2,1)S(1)}, bf16[2,16,17,256]{3,1,2,0:T(8,128)(2,1)}, u32[]{:S(2)}) copy-start(bf16[2,16,17,256]{3,1,2,0:T(8,128)(2,1)} %param.17) | copy-start | bytes 835588
  0.7 35.5 %copy-start.7 = (bf16[256,256]{1,0:T(8,128)(2,1)S(1)}, bf16[256,256]{1,0:T(8,128)(2,1)}, u32[]{:S(2)}) copy-start(bf16[256,256]{1,0:T(8,128)(2,1)} %constant.30.clone.c_ref) | copy-start | bytes 393220
  0.7 35.5 %copy-start.8 = (bf16[256,256]{1,0:T(8,128)(2,1)S(1)}, bf16[256,256]{1,0:T(8,128)(2,1)}, u32[]{:S(2)}) copy-start(bf16[256,256]{1,0:T(8,128)(2,1)} %constant.29.clone.e_ref) | copy-start | bytes 393220
  0.7 35.5 %copy-start.9 = (bf16[128,144]{1,0:T(8,128)(2,1)S(1)}, bf16[128,144]{1,0:T(8,128)(2,1)}, u32[]{:S(2)}) copy-start(bf16[128,144]{1,0:T(8,128)(2,1)} %constant.31.clone.tb_ref) | copy-start | bytes 110596
  36.1 8.3 %copy-start = (bf16[512,512]{1,0:T(8,128)(2,1)S(1)}, bf16[512,512]{1,0:T(8,128)(2,1)}, u32[]{:S(2)}) copy-start(bf16[512,512]{1,0:T(8,128)(2,1)} %constant.32.clone.cut_ref) | copy-start | bytes 1572868
  36.2 15.2 %copy-start.5 = (bf16[128,512]{1,0:T(8,128)(2,1)S(1)}, bf16[128,512]{1,0:T(8,128)(2,1)}, u32[]{:S(2)}) copy-start(bf16[128,512]{1,0:T(8,128)(2,1)} %constant.34.clone.eg_ref) | copy-start | bytes 393220
  36.2 15.2 %copy-start.6 = (bf16[128,512]{1,0:T(8,128)(2,1)S(1)}, bf16[128,512]{1,0:T(8,128)(2,1)}, u32[]{:S(2)}) copy-start(bf16[128,512]{1,0:T(8,128)(2,1)} %constant.33.clone.eu_ref) | copy-start | bytes 393220
  38.3 18.6 %all-to-all-start.1 = ((f32[64,8,128]{2,1,0:T(8,128)}), f32[64,8,128]{2,1,0:T(8,128)S(1)}, u32[]{:S(2)}, u32[]{:S(2)}) async-start(f32[64,8,128]{2,1,0:T(8,128)} %bitcast.5), calls=%async_computation.1 | async-start | bytes 524288 | tf_op jit(solution)/shard_map/all_to_all | solution.py:448
  44.4 12.6 %copy-start.3 = (bf16[256,512]{1,0:T(8,128)(2,1)S(1)}, bf16[256,512]{1,0:T(8,128)(2,1)}, u32[]{:S(2)}) copy-start(bf16[256,512]{1,0:T(8,128)(2,1)} %constant.35.clone.ty_ref) | copy-start | bytes 786436
  44.4 12.5 %copy-start.4 = (bf16[256,192]{1,0:T(8,128)(2,1)S(1)}, bf16[256,192]{1,0:T(8,128)(2,1)}, u32[]{:S(2)}) copy-start(bf16[256,192]{1,0:T(8,128)(2,1)} %constant.36.clone.tx_ref) | copy-start | bytes 294916
  45.0 3.5 %collective-permute-start = (f32[24,256]{1,0:T(8,128)S(1)}, f32[24,256]{1,0:T(8,128)S(1)}, u32[]{:S(2)}, u32[]{:S(2)}) collective-permute-start(f32[24,256]{1,0:T(8,128)S(1)} %get-tuple-element.9), channel_id=1, source_target_pairs={{0,1},{1,0},{2,3},{3,2},{4,5},{5,4},{6,7},{7,6},{8,9},{9,8},{10,11... | collective-permute-start | bytes 73736 | tf_op jit(solution)/shard_map/ppermute | solution.py:458
  45.1 6.1 %collective-permute-start.1 = (f32[24,256]{1,0:T(8,128)S(1)}, f32[24,256]{1,0:T(8,128)S(1)}, u32[]{:S(2)}, u32[]{:S(2)}) collective-permute-start(f32[24,256]{1,0:T(8,128)S(1)} %get-tuple-element.10), channel_id=1, source_target_pairs={{0,2},{1,3},{2,0},{3,1},{4,6},{5,7},{6,4},{7,5},{8,10},{9,11},{10,... | collective-permute-start | bytes 73736 | tf_op jit(solution)/shard_map/ppermute | solution.py:458
  45.9 5.5 %collective-permute-start.2 = (f32[24,256]{1,0:T(8,128)S(1)}, f32[24,256]{1,0:T(8,128)S(1)}, u32[]{:S(2)}, u32[]{:S(2)}) collective-permute-start(f32[24,256]{1,0:T(8,128)S(1)} %get-tuple-element.11), channel_id=1, source_target_pairs={{0,3},{1,2},{2,1},{3,0},{4,7},{5,6},{6,5},{7,4},{8,11},{9,10},{10,... | collective-permute-start | bytes 73736 | tf_op jit(solution)/shard_map/ppermute | solution.py:458

commit v6 on v4

--- a/solution.py
+++ b/solution.py
@@ -386,23 +386,25 @@
         highs.append(grid.astype(bf16).astype(f32))
         lows.append(grid - highs[-1])
     parts = highs + lows
-    place = lane_iota(256, 128) // 32
-
-    def rows_x(c4):
-        moved = [parts[t] if t == c4 else pltpu.roll(parts[t], (t - c4) % 4 * 32, 1) for t in range(4)]
+    def rows_x(c4, start=0, count=8):
+        span = slice(start * 32, (start + count) * 32)
+        moved = [parts[t][span] if t == c4 else pltpu.roll(parts[t][span], (t - c4) % 4 * 32, 1) for t in range(4)]
+        place = lane_iota(count * 32, 128) // 32
         lanes = jnp.where(place == 0, moved[0], jnp.where(place == 1, moved[1], jnp.where(place == 2, moved[2], moved[3])))
         lanes = lanes.astype(bf16)
         high, low = split(dot(jnp.concatenate([lanes, lanes], 1), ty_ref[...]))
-        for pg in range(8):
+        for pg in range(start, start + count):
             for part in range(2):
-                cut = (slice(pg * 32, (pg + 1) * 32), slice(part * 256, (part + 1) * 256))
+                cut = (slice((pg - start) * 32, (pg - start + 1) * 32), slice(part * 256, (part + 1) * 256))
                 q_ref[c4, pg, part * 32:(part + 1) * 32, :] = high[cut]
                 q_ref[c4, pg, 64 + part * 32:64 + (part + 1) * 32, :] = low[cut]
 
-    rows_x(0)
+    rows_x(0, 0, 2)
     for c4 in range(4):
         for pg in range(8):
-            if pg == 1 and c4 < 3:
+            if pg == 1 and c4 == 0:
+                rows_x(0, 2, 6)
+            if pg == 4 and c4 < 3:
                 rows_x(c4 + 1)
             q = q_ref[c4, pg]
             field_ref[pg, c4] = dot(tx_ref[...], jnp.concatenate([q, q[:64]], 0)).astype(bf16)

time: 60 us -> 60 us (level)
  no operation moved by 1% of the time
where the time goes in v6:
time: 60 us; the launch traced here: 59.8 us
  blocking collectives  30 us (50%)
  Pallas kernels  11.5 us (19%)
  starting transfers between devices  9.52 us (16%)
  waiting for transfers between devices  7.86 us (13%)
  between operations  0.78 us (1%)
    all_to_all x1, blocking collectives, exchange(): lax.all_to_all(chunks.reshape(SLABS, rows, 128), 'slab', 0, 0, tiled=True)  30 us
    all_to_all x1, starting transfers between devices, exchange(): lax.all_to_all(chunks.reshape(SLABS, rows, 128), 'slab', 0, 0, tiled=True)  6.06 us
    pallas_call x1, Pallas kernels, forward(): pl.pallas_call(forward_kernel, out_shape=pltpu.VMEM((SLABS * 16, 128), f3...  5.46 us
    all_to_all x1, waiting for transfers between devices, exchange(): lax.all_to_all(chunks.reshape(SLABS, rows, 128), 'slab', 0, 0, tiled=True)  5.02 us
    ppermute x3, starting transfers between devices, body(): pieces[k] = lax.ppermute(pieces[k], 'group', [(i, i ^ k) for i in range(4)])  3.46 us
    ppermute x3, waiting for transfers between devices, body(): pieces[k] = lax.ppermute(pieces[k], 'group', [(i, i ^ k) for i in range(4)])  2.84 us
    pallas_call x1, Pallas kernels, back(): pl.pallas_call(back_kernel, out_shape=(jax.ShapeDtypeStruct((8, 4, NX, NY...  2.81 us
    pallas_call x1, Pallas kernels, middle(): pl.pallas_call(middle_kernel, out_shape=pltpu.VMEM((SLABS * 8, 128), f32)...  2.1 us
  transfers between devices with their start and end apart: 4, of which 3 were waited for; matrix products, arithmetic and copies ran while one was open for 0% of the time, Pallas kernels for 2%

profile of v6, /device:TPU:16, one launch (start us, length us, event | category | flops | bytes accessed | tf_op | source)
XLA Modules:
  0.0 59.8 jit_solution(2274599028549410033)
XLA Ops:
  0.6 0.0 copy-start.1
  0.6 0.0 copy-start.2
  0.7 0.0 copy-start.3
  0.7 0.0 copy-start.8
  0.7 0.0 copy-start.9
  0.7 5.5 %forward_planes.1 = f32[1024,128]{1,0:T(8,128)S(1)} custom-call(bf16[32,256,256]{2,1,0:T(8,128)(2,1)} %bitcast.15, bf16[32,256,256]{2,1,0:T(8,128)(2,1)} %bitcast.16, bf16[128,256]{1,0:T(8,128)(2,1)} %constant.26.clone.tx_hbm, bf16[256,256]{1,0:T(8,128)(2,1)} %constant.27.clone.ty_hbm), custom_call_target="tpu_custom_call" | custom-call | flops 4000000000 | bytes 9000000 | tf_op jit(solution)/shard_map/forward_planes/pallas_call | solution.py:211
  6.2 30.0 %all_to_all.10 = f32[64,16,128]{2,1,0:T(8,128)S(1)} all-to-all(f32[64,16,128]{2,1,0:T(8,128)S(1)} %bitcast.12), channel_id=1, replica_groups=mesh['slab'=64,'group'=4] {'slab'}, dimensions={0} | all-to-all | bytes 1048576 | tf_op jit(solution)/shard_map/all_to_all | solution.py:441
  36.2 0.0 copy-start
  36.2 0.0 copy-done.1
  36.2 0.0 copy-done.2
  36.2 0.0 copy-done.3
  36.2 0.0 copy-done.8
  36.2 0.0 copy-done.9
  36.2 0.0 copy-start.6
  36.2 0.0 copy-start.7
  36.2 2.1 %middle_modes.1 = f32[512,128]{1,0:T(8,128)} custom-call(f32[1024,128]{1,0:T(8,128)S(1)} %bitcast.10, bf16[2,17,16,256]{3,2,1,0:T(8,128)(2,1)S(1)} %bitcast.14, bf16[48,384]{1,0:T(8,128)(2,1)S(1)} %copy-done.1, bf16[256,256]{1,0:T(8,128)(2,1)S(1)} %copy-done.8, bf16[512,512]{1,0:T(8,128)(2,1)S(1)} %copy-done.3, bf16[128,144]{1,0:T(8,128)(2,1)S(1)} %copy-done.9), custom_call_target="tpu_custom_call" | custom-call | flops 2000000000 | bytes 3000000 | tf_op jit(solution)/shard_map/middle_modes/pallas_call | solution.py:300
  38.3 6.1 %all-to-all-start.1 = ((f32[64,8,128]{2,1,0:T(8,128)}), f32[64,8,128]{2,1,0:T(8,128)S(1)}, u32[]{:S(2)}, u32[]{:S(2)}) async-start(f32[64,8,128]{2,1,0:T(8,128)} %bitcast.5), calls=%async_computation.1 | async-start | bytes 524288 | tf_op jit(solution)/shard_map/all_to_all | solution.py:441
  44.4 0.0 copy-done
  44.4 0.0 copy-start.4
  44.4 0.0 copy-start.5
  44.4 0.6 %input_modes.1 = (f32[24,256]{1,0:T(8,128)S(1)}, f32[24,256]{1,0:T(8,128)S(1)}, f32[24,256]{1,0:T(8,128)S(1)}, f32[24,256]{1,0:T(8,128)S(1)}) custom-call(s32[1]{0:T(128)} %bitcast.7.index_ref, f32[1024,128]{1,0:T(8,128)S(1)} %bitcast.11, bf16[48,384]{1,0:T(8,128)(2,1)S(1)} %copy-done.1, bf16[512,512]{1,0:T(8,128)(2,1)S(1)} %copy-done), custom_call_target="tpu_custom_call" | custom-call | flops 100000000 | bytes 1000000 | tf_op jit(solution)/shard_map/input_modes/pallas_call | solution.py:334
  45.0 0.1 collective-permute-start
  45.1 0.7 %collective-permute-start.1 = (f32[24,256]{1,0:T(8,128)S(1)}, f32[24,256]{1,0:T(8,128)S(1)}, u32[]{:S(2)}, u32[]{:S(2)}) collective-permute-start(f32[24,256]{1,0:T(8,128)S(1)} %get-tuple-element.10), channel_id=1, source_target_pairs={{0,2},{1,3},{2,0},{3,1},{4,6},{5,7},{6,4},{7,5},{8,10},{9,11},{10,... | collective-permute-start | bytes 73736 | tf_op jit(solution)/shard_map/ppermute | solution.py:451
  45.9 2.7 %collective-permute-start.2 = (f32[24,256]{1,0:T(8,128)S(1)}, f32[24,256]{1,0:T(8,128)S(1)}, u32[]{:S(2)}, u32[]{:S(2)}) collective-permute-start(f32[24,256]{1,0:T(8,128)S(1)} %get-tuple-element.11), channel_id=1, source_target_pairs={{0,3},{1,2},{2,1},{3,0},{4,7},{5,6},{6,5},{7,4},{8,11},{9,10},{10,... | collective-permute-start | bytes 73736 | tf_op jit(solution)/shard_map/ppermute | solution.py:451
  48.5 0.0 collective-permute-done.b_ref
  48.5 2.7 %collective-permute-done.1.c_ref = f32[24,256]{1,0:T(8,128)S(1)} collective-permute-done((f32[24,256]{1,0:T(8,128)S(1)}, f32[24,256]{1,0:T(8,128)S(1)}, u32[]{:S(2)}, u32[]{:S(2)}) %collective-permute-start.1) | collective-permute-done | bytes 24608 | tf_op jit(solution)/shard_map/ppermute | solution.py:451
  51.2 0.1 collective-permute-done.2.d_ref
  51.3 0.0 copy-done.6
  51.3 0.0 copy-done.7
  51.4 0.6 weight_terms.1.terms_ref
  51.9 5.0 %all-to-all-done.1 = f32[64,8,128]{2,1,0:T(8,128)S(1)} async-done(((f32[64,8,128]{2,1,0:T(8,128)}), f32[64,8,128]{2,1,0:T(8,128)S(1)}, u32[]{:S(2)}, u32[]{:S(2)}) %all-to-all-start.1) | async-done | bytes 262176 | tf_op jit(solution)/shard_map/all_to_all | solution.py:441
  56.9 0.0 copy-done.4
  56.9 0.0 copy-done.5
  56.9 2.8 %back_planes.1 = (bf16[8,4,256,256]{3,2,1,0:T(8,128)(2,1)}, f32[2,17,4,256]{3,2,1,0:T(4,128)}) custom-call(f32[512,128]{1,0:T(8,128)S(1)} %bitcast.13, bf16[256,512]{1,0:T(8,128)(2,1)S(1)} %copy-done.4, bf16[256,192]{1,0:T(8,128)(2,1)S(1)} %copy-done.5, f32[2,17,4,256]{3,2,1,0:T(4,128)S(1)} %weight_terms.1.terms_ref), custom_call_target="tpu_custom_call" | custom-call | flops 4000000000 | bytes 6000000 | tf_op jit(solution)/shard_map/back_planes/pallas_call | solution.py:420
Async XLA Ops:
  0.6 35.5 %copy-start.1 = (bf16[48,384]{1,0:T(8,128)(2,1)S(1)}, bf16[48,384]{1,0:T(8,128)(2,1)}, u32[]{:S(2)}) copy-start(bf16[48,384]{1,0:T(8,128)(2,1)} %constant.28.clone.tz_ref) | copy-start | bytes 110596
  0.6 35.5 %copy-start.2 = (bf16[2,16,17,256]{3,1,2,0:T(8,128)(2,1)S(1)}, bf16[2,16,17,256]{3,1,2,0:T(8,128)(2,1)}, u32[]{:S(2)}) copy-start(bf16[2,16,17,256]{3,1,2,0:T(8,128)(2,1)} %param.17) | copy-start | bytes 835588
  0.7 35.5 %copy-start.3 = (bf16[512,512]{1,0:T(8,128)(2,1)S(1)}, bf16[512,512]{1,0:T(8,128)(2,1)}, u32[]{:S(2)}) copy-start(bf16[512,512]{1,0:T(8,128)(2,1)} %constant.30.clone.c_ref) | copy-start | bytes 1572868
  0.7 35.5 %copy-start.8 = (bf16[256,256]{1,0:T(8,128)(2,1)S(1)}, bf16[256,256]{1,0:T(8,128)(2,1)}, u32[]{:S(2)}) copy-start(bf16[256,256]{1,0:T(8,128)(2,1)} %constant.29.clone.e_ref) | copy-start | bytes 393220
  0.7 35.5 %copy-start.9 = (bf16[128,144]{1,0:T(8,128)(2,1)S(1)}, bf16[128,144]{1,0:T(8,128)(2,1)}, u32[]{:S(2)}) copy-start(bf16[128,144]{1,0:T(8,128)(2,1)} %constant.31.clone.tb_ref) | copy-start | bytes 110596
  36.2 8.2 %copy-start = (bf16[512,512]{1,0:T(8,128)(2,1)S(1)}, bf16[512,512]{1,0:T(8,128)(2,1)}, u32[]{:S(2)}) copy-start(bf16[512,512]{1,0:T(8,128)(2,1)} %constant.32.clone.cut_ref) | copy-start | bytes 1572868
  36.2 15.2 %copy-start.6 = (bf16[128,512]{1,0:T(8,128)(2,1)S(1)}, bf16[128,512]{1,0:T(8,128)(2,1)}, u32[]{:S(2)}) copy-start(bf16[128,512]{1,0:T(8,128)(2,1)} %constant.34.clone.eg_ref) | copy-start | bytes 393220
  36.2 15.1 %copy-start.7 = (bf16[128,512]{1,0:T(8,128)(2,1)S(1)}, bf16[128,512]{1,0:T(8,128)(2,1)}, u32[]{:S(2)}) copy-start(bf16[128,512]{1,0:T(8,128)(2,1)} %constant.33.clone.eu_ref) | copy-start | bytes 393220
  38.3 18.6 %all-to-all-start.1 = ((f32[64,8,128]{2,1,0:T(8,128)}), f32[64,8,128]{2,1,0:T(8,128)S(1)}, u32[]{:S(2)}, u32[]{:S(2)}) async-start(f32[64,8,128]{2,1,0:T(8,128)} %bitcast.5), calls=%async_computation.1 | async-start | bytes 524288 | tf_op jit(solution)/shard_map/all_to_all | solution.py:441
  44.4 12.6 %copy-start.4 = (bf16[256,512]{1,0:T(8,128)(2,1)S(1)}, bf16[256,512]{1,0:T(8,128)(2,1)}, u32[]{:S(2)}) copy-start(bf16[256,512]{1,0:T(8,128)(2,1)} %constant.35.clone.ty_ref) | copy-start | bytes 786436
  44.4 12.5 %copy-start.5 = (bf16[256,192]{1,0:T(8,128)(2,1)S(1)}, bf16[256,192]{1,0:T(8,128)(2,1)}, u32[]{:S(2)}) copy-start(bf16[256,192]{1,0:T(8,128)(2,1)} %constant.36.clone.tx_ref) | copy-start | bytes 294916
  45.0 3.5 %collective-permute-start = (f32[24,256]{1,0:T(8,128)S(1)}, f32[24,256]{1,0:T(8,128)S(1)}, u32[]{:S(2)}, u32[]{:S(2)}) collective-permute-start(f32[24,256]{1,0:T(8,128)S(1)} %get-tuple-element.9), channel_id=1, source_target_pairs={{0,1},{1,0},{2,3},{3,2},{4,5},{5,4},{6,7},{7,6},{8,9},{9,8},{10,11... | collective-permute-start | bytes 73736 | tf_op jit(solution)/shard_map/ppermute | solution.py:451
  45.1 6.1 %collective-permute-start.1 = (f32[24,256]{1,0:T(8,128)S(1)}, f32[24,256]{1,0:T(8,128)S(1)}, u32[]{:S(2)}, u32[]{:S(2)}) collective-permute-start(f32[24,256]{1,0:T(8,128)S(1)} %get-tuple-element.10), channel_id=1, source_target_pairs={{0,2},{1,3},{2,0},{3,1},{4,6},{5,7},{6,4},{7,5},{8,10},{9,11},{10,... | collective-permute-start | bytes 73736 | tf_op jit(solution)/shard_map/ppermute | solution.py:451
  45.9 5.5 %collective-permute-start.2 = (f32[24,256]{1,0:T(8,128)S(1)}, f32[24,256]{1,0:T(8,128)S(1)}, u32[]{:S(2)}, u32[]{:S(2)}) collective-permute-start(f32[24,256]{1,0:T(8,128)S(1)} %get-tuple-element.11), channel_id=1, source_target_pairs={{0,3},{1,2},{2,1},{3,0},{4,7},{5,6},{6,5},{7,4},{8,11},{9,10},{10,... | collective-permute-start | bytes 73736 | tf_op jit(solution)/shard_map/ppermute | solution.py:451
